TPU v7x, 128 devices: a whole 4x4x4 slice. The times are simulated.
128 devices in a mesh: seq: 64 (over z, x, y), tensor: 2 (over core).
Axes of the slice: x: 4, y: 4, z: 4, core: 2. Of those that a mesh axis runs over, the one named last changes fastest.
Arguments:
- tokens: bfloat16 [8192, 1536], P('seq'), may hold values from -6 to 6
- cotangent: bfloat16 [8192, 1536], P('seq'), may hold values from -6 to 6
- lengths: int32 [8], replicated, may hold values from 200 to 4096, as said below
- norm1_gain: float32 [1536], replicated, may hold values from 0.5 to 1.5
- w_query: bfloat16 [1536, 12, 128], P(None, 'tensor'), may hold values from -0.15625 to 0.15625
- b_query: bfloat16 [12, 128], P('tensor'), may hold values from -3 to 3
- w_key: bfloat16 [1536, 2, 128], P(None, 'tensor'), may hold values from -0.15625 to 0.15625
- b_key: bfloat16 [2, 128], P('tensor'), may hold values from -3 to 3
- w_value: bfloat16 [1536, 2, 128], P(None, 'tensor'), may hold values from -0.15625 to 0.15625
- b_value: bfloat16 [2, 128], P('tensor'), may hold values from -3 to 3
- w_out: bfloat16 [12, 128, 1536], P('tensor'), may hold values from -1.25 to 1.25
- norm2_gain: float32 [1536], replicated, may hold values from 0.5 to 1.5
- w_gate: bfloat16 [1536, 8960], P(None, 'tensor'), may hold values from -0.15625 to 0.15625
- w_up: bfloat16 [1536, 8960], P(None, 'tensor'), may hold values from -0.15625 to 0.15625
- w_down: bfloat16 [8960, 1536], P('tensor'), may hold values from -0.25 to 0.25
Outputs:
- output: float32 [8192, 1536], P('seq')
- grad_tokens: float32 [8192, 1536], P('seq')
- grad_norm1: float32 [1536], P('seq')
- grad_w_query: float32 [1536, 12, 128], P('seq', 'tensor')
- grad_b_query: float32 [12, 128], P('tensor', 'seq')
- grad_w_key: float32 [1536, 2, 128], P('seq', 'tensor')
- grad_b_key: float32 [2, 128], P('tensor', 'seq')
- grad_w_value: float32 [1536, 2, 128], P('seq', 'tensor')
- grad_b_value: float32 [2, 128], P('tensor', 'seq')
- grad_w_out: float32 [12, 128, 1536], P('tensor', None, 'seq')
- grad_norm2: float32 [1536], P('seq')
- grad_w_gate: float32 [1536, 8960], P('seq', 'tensor')
- grad_w_up: float32 [1536, 8960], P('seq', 'tensor')
- grad_w_down: float32 [8960, 1536], P('tensor', 'seq')
Inputs may be any that keep to these rules, and one draw needn't show every extreme that they name: The 8 lengths sum to 8192; each is at least 200; exactly one, at a place in the pack drawn from the seed, is 4096 long, and all others are shorter.
All inputs are finite; a program needn't handle non-finite values.
Results may differ from a plain program's by a relative error of at most 0.035.
Values may be sent and summed in bfloat16 or wider, within the bound.
A program may use at most 320 MiB of HBM per device.

v0:
```python
import math

import jax
import jax.numpy as jnp
from jax import lax
from jax.sharding import PartitionSpec as P


def inverse_rms(values):
    return lax.rsqrt(jnp.mean(values * values, axis=-1, keepdims=True) + 1e-06)


def rotate(values, cos_table, sin_table):
    half_dim = values.shape[-1] // 2
    front = values[..., :half_dim]
    back_half = values[..., half_dim:]
    return jnp.concatenate(
        [front * cos_table - back_half * sin_table, back_half * cos_table + front * sin_table],
        axis=-1,
    )


def rotate_back(gradient, cos_table, sin_table):
    half_dim = gradient.shape[-1] // 2
    front = gradient[..., :half_dim]
    back_half = gradient[..., half_dim:]
    return jnp.concatenate(
        [front * cos_table + back_half * sin_table, back_half * cos_table - front * sin_table],
        axis=-1,
    )


def locate(positions, doc_ends, lengths):
    is_past = positions[:, None] >= doc_ends[None, :]
    doc_ids = jnp.sum(is_past.astype(jnp.int32), axis=1)
    doc_start = jnp.sum(jnp.where(is_past, lengths[None, :], 0), axis=1)
    return (doc_ids, doc_start)


def norm_back(gradient, source, inverse, gain):
    scaled = gradient * gain
    gain_grad = jnp.sum(gradient * source * inverse, axis=0)
    source_grad = inverse * scaled - source * inverse**3 * jnp.mean(
        scaled * source, axis=-1, keepdims=True
    )
    return (source_grad, gain_grad)


def local(
    tokens,
    cotangent,
    lengths,
    norm1_gain,
    w_query,
    b_query,
    w_key,
    b_key,
    w_value,
    b_value,
    w_out,
    norm2_gain,
    w_gate,
    w_up,
    w_down,
):
    tok_rows = tokens.shape[0]
    num_heads = w_query.shape[1]
    head_dim = w_query.shape[2]
    kv_local = w_key.shape[1]
    group = num_heads // kv_local
    half_dim = head_dim // 2
    score_scale = 1.0 / math.sqrt(head_dim)
    seq_count = lax.axis_size("seq")
    device = lax.axis_index("seq")
    positions = jnp.arange(tok_rows, dtype=jnp.int32) * seq_count + device
    doc_ends = jnp.cumsum(lengths)
    doc_ids, doc_start = locate(positions, doc_ends, lengths)
    rel_pos = (positions - doc_start).astype(jnp.float32)
    inv_freq = jnp.exp(
        -(2.0 * jnp.arange(half_dim, dtype=jnp.float32) / head_dim) * math.log(10000.0)
    )
    angles = rel_pos[:, None] * inv_freq[None, :]
    cos_table = jnp.cos(angles)[:, None, :]
    sin_table = jnp.sin(angles)[:, None, :]
    inputs = tokens.astype(jnp.float32)
    inv_first = inverse_rms(inputs)
    normed_first = (inputs * inv_first * norm1_gain).astype(jnp.bfloat16)
    q_pre = jnp.einsum(
        "td,dhe->the", normed_first, w_query, preferred_element_type=jnp.float32
    ) + b_query.astype(jnp.float32)
    k_pre = jnp.einsum(
        "td,dhe->the", normed_first, w_key, preferred_element_type=jnp.float32
    ) + b_key.astype(jnp.float32)
    v_pre = jnp.einsum(
        "td,dhe->the", normed_first, w_value, preferred_element_type=jnp.float32
    ) + b_value.astype(jnp.float32)
    query_rows = (
        rotate(q_pre, cos_table, sin_table)
        .astype(jnp.bfloat16)
        .reshape(tok_rows, kv_local, group, head_dim)
    )
    key_rows = rotate(k_pre, cos_table, sin_table).astype(jnp.bfloat16)
    value_rows = v_pre.astype(jnp.bfloat16)
    all_key, all_value = (
        lax.all_gather(key_rows, "seq", axis=0, tiled=True),
        lax.all_gather(value_rows, "seq", axis=0, tiled=True),
    )
    key_total = all_key.shape[0]
    key_block = min(512, key_total)
    block_count = key_total // key_block

    def block_scores(blk_index, keys_all):
        start = blk_index * key_block
        key_blk = lax.dynamic_slice_in_dim(keys_all, start, key_block, 0)
        scores = (
            jnp.einsum("tkgd,skd->tkgs", query_rows, key_blk, preferred_element_type=jnp.float32)
            * score_scale
        )
        key_row = start + jnp.arange(key_block, dtype=jnp.int32)
        key_pos = key_row % tok_rows * seq_count + key_row // tok_rows
        key_doc, unused_start = locate(key_pos, doc_ends, lengths)
        visible = (key_doc[None, :] == doc_ids[:, None]) & (key_pos[None, :] <= positions[:, None])
        return (scores, visible[:, None, None, :], start, key_blk)

    def lse_step(blk_index, carried):
        row_max, row_sum = carried
        scores, visible, start, key_blk = block_scores(blk_index, all_key)
        new_max = jnp.maximum(row_max, jnp.max(jnp.where(visible, scores, -1e30), axis=-1))
        expon = jnp.where(visible, jnp.exp(scores - new_max[..., None]), 0.0)
        return (new_max, row_sum * jnp.exp(row_max - new_max) + jnp.sum(expon, axis=-1))

    stat_shape = (tok_rows, kv_local, group)
    row_max, row_sum = lax.fori_loop(
        0,
        block_count,
        lse_step,
        (jnp.full(stat_shape, -1e30, jnp.float32), jnp.zeros(stat_shape, jnp.float32)),
    )
    log_norm = row_max + jnp.log(row_sum)

    def out_step(blk_index, out_acc):
        scores, visible, start, key_blk = block_scores(blk_index, all_key)
        val_blk = lax.dynamic_slice_in_dim(all_value, start, key_block, 0)
        probs_low = jnp.where(visible, jnp.exp(scores - log_norm[..., None]), 0.0).astype(
            jnp.bfloat16
        )
        return out_acc + jnp.einsum(
            "tkgs,skd->tkgd", probs_low, val_blk, preferred_element_type=jnp.float32
        )

    attn_float = lax.fori_loop(
        0, block_count, out_step, jnp.zeros((tok_rows, kv_local, group, head_dim), jnp.float32)
    )
    attn_low = attn_float.astype(jnp.bfloat16).reshape(tok_rows, num_heads, head_dim)
    branch_part = jnp.einsum("the,hed->td", attn_low, w_out, preferred_element_type=jnp.float32)
    mid_stream = inputs + lax.psum(branch_part, "tensor")
    inv_second = inverse_rms(mid_stream)
    normed_second = (mid_stream * inv_second * norm2_gain).astype(jnp.bfloat16)
    gate_act = jnp.dot(normed_second, w_gate, preferred_element_type=jnp.float32)
    up_act = jnp.dot(normed_second, w_up, preferred_element_type=jnp.float32)
    sigma_gate = jax.nn.sigmoid(gate_act)
    silu_gate = gate_act * sigma_gate
    hidden = (silu_gate * up_act).astype(jnp.bfloat16)
    mlp_part = jnp.dot(hidden, w_down, preferred_element_type=jnp.float32)
    output = mid_stream + lax.psum(mlp_part, "tensor")
    g_hidden = jnp.einsum("td,fd->tf", cotangent, w_down, preferred_element_type=jnp.float32)
    d_w_down = jnp.einsum("tf,td->fd", hidden, cotangent, preferred_element_type=jnp.float32)
    g_gate = (g_hidden * up_act * sigma_gate * (1.0 + gate_act * (1.0 - sigma_gate))).astype(
        jnp.bfloat16
    )
    g_up = (g_hidden * silu_gate).astype(jnp.bfloat16)
    d_w_gate = jnp.einsum("td,tf->df", normed_second, g_gate, preferred_element_type=jnp.float32)
    d_w_up = jnp.einsum("td,tf->df", normed_second, g_up, preferred_element_type=jnp.float32)
    g_normed2_part = jnp.einsum(
        "tf,df->td", g_gate, w_gate, preferred_element_type=jnp.float32
    ) + jnp.einsum("tf,df->td", g_up, w_up, preferred_element_type=jnp.float32)
    g_normed2 = lax.psum(g_normed2_part, "tensor")
    g_mid_norm, d_norm2 = norm_back(g_normed2, mid_stream, inv_second, norm2_gain)
    g_mid = cotangent.astype(jnp.float32) + g_mid_norm
    mlp_sent = (
        lax.psum_scatter(d_w_gate, "seq", scatter_dimension=0, tiled=True),
        lax.psum_scatter(d_w_up, "seq", scatter_dimension=0, tiled=True),
        lax.psum_scatter(d_w_down, "seq", scatter_dimension=1, tiled=True),
        lax.psum_scatter(d_norm2, "seq", scatter_dimension=0, tiled=True),
    )
    g_branch = g_mid.astype(jnp.bfloat16)
    d_w_out = jnp.einsum("the,td->hed", attn_low, g_branch, preferred_element_type=jnp.float32)
    g_attn = (
        jnp.einsum("td,hed->the", g_branch, w_out, preferred_element_type=jnp.float32)
        .astype(jnp.bfloat16)
        .reshape(tok_rows, kv_local, group, head_dim)
    )
    back_key, back_value = (
        lax.all_gather(key_rows, "seq", axis=0, tiled=True),
        lax.all_gather(value_rows, "seq", axis=0, tiled=True),
    )

    def delta_step(blk_index, delta_acc):
        scores, visible, start, key_blk = block_scores(blk_index, back_key)
        val_blk = lax.dynamic_slice_in_dim(back_value, start, key_block, 0)
        probs = jnp.where(visible, jnp.exp(scores - log_norm[..., None]), 0.0)
        g_probs = jnp.einsum("tkgd,skd->tkgs", g_attn, val_blk, preferred_element_type=jnp.float32)
        return delta_acc + jnp.sum(probs * g_probs, axis=-1)

    delta = lax.fori_loop(0, block_count, delta_step, jnp.zeros(stat_shape, jnp.float32))

    def back_step(blk_index, carried):
        dq_acc, dk_acc, dv_acc = carried
        scores, visible, start, key_blk = block_scores(blk_index, back_key)
        val_blk = lax.dynamic_slice_in_dim(back_value, start, key_block, 0)
        probs = jnp.where(visible, jnp.exp(scores - log_norm[..., None]), 0.0)
        probs_low = probs.astype(jnp.bfloat16)
        g_probs = jnp.einsum("tkgd,skd->tkgs", g_attn, val_blk, preferred_element_type=jnp.float32)
        g_scores = (probs * (g_probs - delta[..., None])).astype(jnp.bfloat16)
        dq_acc = dq_acc + jnp.einsum(
            "tkgs,skd->tkgd", g_scores, key_blk, preferred_element_type=jnp.float32
        )
        dk_blk = (
            jnp.einsum("tkgs,tkgd->skd", g_scores, query_rows, preferred_element_type=jnp.float32)
            * score_scale
        )
        dv_blk = jnp.einsum("tkgs,tkgd->skd", probs_low, g_attn, preferred_element_type=jnp.float32)
        dk_acc = lax.dynamic_update_slice_in_dim(dk_acc, dk_blk, start, 0)
        dv_acc = lax.dynamic_update_slice_in_dim(dv_acc, dv_blk, start, 0)
        return (dq_acc, dk_acc, dv_acc)

    kv_zeros = jnp.zeros((key_total, kv_local, head_dim), jnp.float32)
    dq_acc, dk_acc, dv_acc = lax.fori_loop(
        0,
        block_count,
        back_step,
        (jnp.zeros((tok_rows, kv_local, group, head_dim), jnp.float32), kv_zeros, kv_zeros),
    )
    dk_own, dv_own = (
        lax.psum_scatter(dk_acc, "seq", scatter_dimension=0, tiled=True),
        lax.psum_scatter(dv_acc, "seq", scatter_dimension=0, tiled=True),
    )
    g_q_pre = rotate_back(
        dq_acc.reshape(tok_rows, num_heads, head_dim) * score_scale, cos_table, sin_table
    ).astype(jnp.bfloat16)
    g_k_pre = rotate_back(dk_own, cos_table, sin_table).astype(jnp.bfloat16)
    g_v_pre = dv_own.astype(jnp.bfloat16)
    d_w_query = jnp.einsum("td,the->dhe", normed_first, g_q_pre, preferred_element_type=jnp.float32)
    d_w_key = jnp.einsum("td,the->dhe", normed_first, g_k_pre, preferred_element_type=jnp.float32)
    d_w_value = jnp.einsum("td,the->dhe", normed_first, g_v_pre, preferred_element_type=jnp.float32)
    d_b_query = jnp.sum(g_q_pre.astype(jnp.float32), axis=0)
    d_b_key = jnp.sum(g_k_pre.astype(jnp.float32), axis=0)
    d_b_value = jnp.sum(g_v_pre.astype(jnp.float32), axis=0)
    g_normed1_part = jnp.einsum("the,dhe->td", g_q_pre, w_query, preferred_element_type=jnp.float32)
    g_normed1_part = g_normed1_part + jnp.einsum(
        "the,dhe->td", g_k_pre, w_key, preferred_element_type=jnp.float32
    )
    g_normed1_part = g_normed1_part + jnp.einsum(
        "the,dhe->td", g_v_pre, w_value, preferred_element_type=jnp.float32
    )
    g_normed1 = lax.psum(g_normed1_part, "tensor")
    g_input_norm, d_norm1 = norm_back(g_normed1, inputs, inv_first, norm1_gain)
    grad_tokens = g_mid + g_input_norm
    attn_sent = (
        lax.psum_scatter(d_w_query, "seq", scatter_dimension=0, tiled=True),
        lax.psum_scatter(d_w_key, "seq", scatter_dimension=0, tiled=True),
        lax.psum_scatter(d_w_value, "seq", scatter_dimension=0, tiled=True),
        lax.psum_scatter(d_w_out, "seq", scatter_dimension=2, tiled=True),
        lax.psum_scatter(d_b_query, "seq", scatter_dimension=1, tiled=True),
        lax.psum_scatter(d_b_key, "seq", scatter_dimension=1, tiled=True),
        lax.psum_scatter(d_b_value, "seq", scatter_dimension=1, tiled=True),
        lax.psum_scatter(d_norm1, "seq", scatter_dimension=0, tiled=True),
    )
    grad_gate, grad_up, grad_down, grad_norm2 = mlp_sent
    grad_wq, grad_wk, grad_wv, grad_wo, grad_bq, grad_bk, grad_bv, grad_norm1 = attn_sent
    return (
        output,
        grad_tokens,
        grad_norm1,
        grad_wq,
        grad_bq,
        grad_wk,
        grad_bk,
        grad_wv,
        grad_bv,
        grad_wo,
        grad_norm2,
        grad_gate,
        grad_up,
        grad_down,
    )


def solution(mesh):
    in_specs = (
        P("seq", None),
        P("seq", None),
        P(),
        P(),
        P(None, "tensor", None),
        P("tensor", None),
        P(None, "tensor", None),
        P("tensor", None),
        P(None, "tensor", None),
        P("tensor", None),
        P("tensor", None, None),
        P(),
        P(None, "tensor"),
        P(None, "tensor"),
        P("tensor", None),
    )
    out_specs = (
        P("seq", None),
        P("seq", None),
        P("seq"),
        P("seq", "tensor", None),
        P("tensor", "seq"),
        P("seq", "tensor", None),
        P("tensor", "seq"),
        P("seq", "tensor", None),
        P("tensor", "seq"),
        P("tensor", None, "seq"),
        P("seq"),
        P("seq", "tensor"),
        P("seq", "tensor"),
        P("tensor", "seq"),
    )
    return jax.shard_map(local, mesh=mesh, in_specs=in_specs, out_specs=out_specs, check_vma=False)
```

profile of v0, /device:TPU:0, one launch (start us, length us, event | category | flops | bytes accessed | tf_op | source)
XLA Modules:
  0.0 2873.0 jit_solution(12907791013274237053)
XLA Ops:
  16.9 4.3 copy.79
  21.2 2.5 fusion.145
  25.7 57.7 %all-gather.4.cloned.1.call-done = bf16[8192,1,128]{0,2,1:T(8,128)(2,1)} async-done(((bf16[128,1,128]{0,2,1:T(8,128)(2,1)}), bf16[8192,1,128]{0,2,1:T(8,128)(2,1)}) %all-gather.4.cloned.1.call-update) | async-done | bytes 2097168 | tf_op jit(solution)/shard_map/all_gather | solution.py:105
  83.5 4.1 copy.83
  87.6 31.8 %while.70 = (s32[]{:T(128)}, f32[128,1,6]{0,2,1:T(8,128)S(1)}, f32[128,1,6]{0,2,1:T(8,128)S(1)}, s32[8]{0:T(128)S(1)}, s32[128]{0:T(128)S(1)}, /*index=5*/bf16[8...) while((s32[]{:T(128)}, f32[128,1,6]{0,2,1:T(8,128)S(1)}, ...), condition=%wide.region_8.9_spmd.clone, body=%wide.region_4.8_spmd.clone.sunk | while | flops 103246344 | bytes 3721954 | solution.py:133
  119.4 32.5 %all-gather.6.cloned.1.call-done = bf16[8192,128]{1,0:T(8,128)(2,1)} async-done(((bf16[128,128]{1,0:T(8,128)(2,1)}), bf16[8192,128]{1,0:T(8,128)(2,1)}) %all-gather.6.cloned.1.call-update) | async-done | bytes 2097168 | tf_op jit(solution)/shard_map/all_gather | solution.py:106
  151.9 33.0 %while.71 = (s32[]{:T(128)}, f32[128,1,6,128]{0,3,2,1:T(8,128)S(1)}, bf16[8192,1,128]{2,0,1:T(8,128)(2,1)}, s32[8]{0:T(128)S(1)}, s32[128]{0:T(128)S(1)}, /*inde...) while((s32[]{:T(128)}, ...), condition=%wide.region_11.12_spmd.clone, body=%wide.region_9.11_spmd.clone.sunk | while | flops 203315968 | bytes 1392868 | solution.py:151
  186.5 22.2 all-reduce.16.cloned.1.call-done
  211.1 8.5 fusion.150
  219.6 8.5 fusion.149
  228.1 12.1 multiply_convert_fusion
  240.3 10.1 fusion.152
  250.4 10.3 convolution_add_fusion.2
  261.0 26.0 all-reduce.18.cloned.1.call-done
  290.9 49.2 %while.72 = (s32[]{:T(128)}, f32[128,1,6]{0,1,2:T(1,128)S(1)}, s32[8]{0:T(128)S(1)}, s32[128]{0:T(128)S(1)}, bf16[8192,1,128]{2,0,1:T(8,128)(2,1)}, /*index=5*/b...) while((s32[]{:T(128)}, f32[128,1,6]{0,1,2:T(1,128)S(1)}, ...), condition=%wide.region_20.21_spmd.clone, body=%wide.region_17.20_spmd.clone.sunk | while | flops 203513344 | bytes 3959541 | solution.py:205
  340.1 2.2 broadcast_in_dim.259
  342.4 2.4 broadcast_in_dim.259.clone
  344.8 119.2 %while.73 = (s32[]{:T(128)}, f32[128,1,6,128]{0,3,2,1:T(8,128)}, f32[8192,1,128]{0,2,1:T(8,128)}, f32[8192,1,128]{2,0,1:T(8,128)}, bf16[8192,1,128]{2,0,1:T(8,12...) while((s32[]{:T(128)}, f32[128,1,6,128]{0,3,2,1:T(8,128)}, ...), condition=%wide.region_23.24_spmd.clone, body=%wide.region_21.23_spmd.clone.sunk | while | flops 506551040 | bytes 10766105 | solution.py:228
  355.4 2.1 fusion.239
  362.9 2.1 fusion.239
  370.4 2.1 fusion.239
  377.8 2.1 fusion.239
  385.3 2.1 fusion.239
  392.7 2.1 fusion.239
  400.2 2.1 fusion.239
  422.5 2.1 fusion.239
  430.0 2.1 fusion.239
  437.4 2.1 fusion.239
  444.9 2.1 fusion.239
  452.3 2.1 fusion.239
  459.8 2.1 fusion.239
  464.6 8.3 fusion.151
  475.6 347.7 %reduce-scatter.24.cloned.1.call-done = f32[128,1,128]{0,2,1:T(8,128)} async-done(((f32[8192,1,128]{0,2,1:T(8,128)}), f32[128,1,128]{0,2,1:T(8,128)}) %reduce-scatter.24.cloned.1.call-update) | async-done | bytes 65552 | tf_op jit(solution)/shard_map/reduce_scatter | solution.py:235
  826.2 351.9 %reduce-scatter.26.cloned.1.call-done = f32[128,1,128]{2,0,1:T(8,128)} async-done(((f32[8192,1,128]{2,0,1:T(8,128)}), f32[128,1,128]{2,0,1:T(8,128)}) %reduce-scatter.26.cloned.1.call-update) | async-done | bytes 65552 | tf_op jit(solution)/shard_map/reduce_scatter | solution.py:236
  1180.1 3.0 fusion.101
  1184.1 3.0 fusion.99
  1190.6 11.5 fusion.155
  1203.5 11.0 fusion.154
  1215.8 11.2 fusion.153
  1231.5 2.3 add.712
  1234.7 342.4 %all-reduce.10 = (f32[1536]{0:T(1024)S(1)}, f32[6,128]{0,1:T(8,128)S(1)}, f32[1,128]{1,0:T(1,128)S(1)}, f32[1,128]{1,0:T(1,128)S(1)}, f32[1536]{0:T(1024)S(1)}) all-reduce(f32[1536]{0:T(1024)S(1)} %get-tuple-element.1312, f32[6,128]{0,1:T(8,128)} %copy.95, ...), channel_id=5, replica_groups=mesh['seq'=64,'tensor'=2] {'seq'}, use_global_device_ids=true, to_apply=%region_29.30.clone | all-reduce | flops 4096 | bytes 32768
  1579.4 2.6 fusion.95
  1582.0 73.5 %reduce-scatter.28.cloned.1.call-done = f32[24,6,128]{2,0,1:T(8,128)} async-done(((f32[1536,6,128]{2,0,1:T(8,128)}), f32[24,6,128]{2,0,1:T(8,128)}) %reduce-scatter.28.cloned.1.call-update) | async-done | bytes 73744 | tf_op jit(solution)/shard_map/reduce_scatter | solution.py:260
  1655.5 220.3 %reduce-scatter.34.cloned.1.call-done = f32[24,1,128]{2,0,1:T(8,128)} async-done(((f32[1536,1,128]{2,0,1:T(8,128)}), f32[24,1,128]{2,0,1:T(8,128)}) %reduce-scatter.34.cloned.1.call-update) | async-done | bytes 12304
  1875.7 220.4 %reduce-scatter.32.cloned.1.call-done = f32[24,1,128]{2,0,1:T(8,128)} async-done(((f32[1536,1,128]{2,0,1:T(8,128)}), f32[24,1,128]{2,0,1:T(8,128)}) %reduce-scatter.32.cloned.1.call-update) | async-done | bytes 12304
  2096.2 256.9 %reduce-scatter.40.cloned.1.call-done = f32[4480,24]{0,1:T(8,128)} async-done(((f32[4480,1536]{0,1:T(8,128)}), f32[4480,24]{0,1:T(8,128)}) %reduce-scatter.40.cloned.1.call-update) | async-done | bytes 430096
  2353.1 256.8 %reduce-scatter.38.cloned.1.call-done = f32[24,4480]{1,0:T(8,128)} async-done(((f32[1536,4480]{1,0:T(8,128)}), f32[24,4480]{1,0:T(8,128)}) %reduce-scatter.38.cloned.1.call-update) | async-done | bytes 430096
  2609.9 256.6 %reduce-scatter.36.cloned.1.call-done = f32[24,4480]{1,0:T(8,128)} async-done(((f32[1536,4480]{1,0:T(8,128)}), f32[24,4480]{1,0:T(8,128)}) %reduce-scatter.36.cloned.1.call-update) | async-done | bytes 430096
  (660 shorter events, 243.4 us)
Async XLA Ops:
  7.2 177.7 %copy-start = (bf16[6,128,1536]{2,1,0:T(8,128)(2,1)S(1)}, bf16[6,128,1536]{2,1,0:T(8,128)(2,1)}, u32[]{:S(2)}) copy-start(bf16[6,128,1536]{2,1,0:T(8,128)(2,1)} %param.33) | copy-start | bytes 7077892
  7.2 9.6 copy-start.37
  7.2 76.3 %all-gather.4.cloned.1.call-start = ((), (), s32[]{:S(2)}) async-start(), calls=%async_computation.9 | async-start | bytes 2129920 | tf_op jit(solution)/shard_map/all_gather | solution.py:105
  7.3 9.5 copy-start.35
  10.8 10.4 copy-start.36
  11.4 9.8 copy-start.33
  13.7 138.2 %all-gather.6.cloned.1.call-start = ((), (), s32[]{:S(2)}) async-start(), calls=%async_computation.16 | async-start | bytes 2129920 | tf_op jit(solution)/shard_map/all_gather | solution.py:106
  16.5 192.2 %all-reduce.16.cloned.1.call-start = ((), (), s32[]{:S(2)}) async-start(), calls=%async_computation.10 | async-start | bytes 1572864 | tf_op jit(solution)/shard_map/psum | solution.py:156
  16.8 4.4 copy-start.2
  16.8 4.4 copy-start.27
  184.9 1.4 copy-start.19
  186.3 24.7 copy-start.32
  186.3 100.7 %all-reduce.18.cloned.1.call-start = ((), (), s32[]{:S(2)}) async-start(), calls=%async_computation.11 | async-start | bytes 1572864 | tf_op jit(solution)/shard_map/psum | solution.py:177
  210.1 0.9 copy-start.3
  211.1 8.6 copy-start.6
  219.6 8.5 copy-start.17
  240.3 10.1 copy-start.12
  260.7 562.5 %reduce-scatter.24.cloned.1.call-start = ((), (), s32[]{:S(2)}) async-start(), calls=%async_computation.12 | async-start | bytes 4259840 | tf_op jit(solution)/shard_map/reduce_scatter | solution.py:235
  287.0 1.7 copy-start.4
  287.0 1.8 copy-start.16
  289.1 0.9 copy-start.8
  463.9 714.1 %reduce-scatter.26.cloned.1.call-start = ((), (), s32[]{:S(2)}) async-start(), calls=%async_computation.13 | async-start | bytes 4259840 | tf_op jit(solution)/shard_map/reduce_scatter | solution.py:236
  464.5 767.0 %all-reduce.20.cloned.1.call-start = ((), (), s32[]{:S(2)}) async-start(), calls=%async_computation.22 | async-start | bytes 3145728 | tf_op jit(solution)/shard_map/psum | solution.py:165
  464.6 10.1 copy-start.10
  475.5 702.5 %copy-start.26 = (bf16[1536,1,128]{2,0,1:T(8,128)(2,1)S(1)}, bf16[1536,1,128]{2,0,1:T(8,128)(2,1)}, u32[]{:S(2)}) copy-start(bf16[1536,1,128]{2,0,1:T(8,128)(2,1)} %param.31) | copy-start | bytes 1179652
  826.1 354.0 %copy-start.9 = (f32[128,1536]{1,0:T(8,128)S(1)}, f32[128,1536]{1,0:T(8,128)}, u32[]{:S(2)}) copy-start(f32[128,1536]{1,0:T(8,128)} %copy-done.8) | copy-start | bytes 2359300
  826.2 354.0 %copy-start.20 = (f32[128,1,6,128]{0,3,2,1:T(8,128)S(1)}, f32[128,1,6,128]{0,3,2,1:T(8,128)}, u32[]{:S(2)}) copy-start(f32[128,1,6,128]{0,3,2,1:T(8,128)} %copy-done.19) | copy-start | bytes 1179652
  1180.1 402.0 %reduce-scatter.30.cloned.1.call-start = ((), (), s32[]{:S(2)}) async-start(), calls=%async_computation.15 | async-start | bytes 4792320 | tf_op jit(solution)/shard_map/reduce_scatter | solution.py:263
  1183.1 0.9 copy-start.22
  1183.1 0.9 copy-start.24
  1183.1 0.9 copy-start.34
  1183.1 472.3 %reduce-scatter.28.cloned.1.call-start = ((), (), s32[]{:S(2)}) async-start(), calls=%async_computation.14 | async-start | bytes 4792320 | tf_op jit(solution)/shard_map/reduce_scatter | solution.py:260
  1187.0 0.8 copy-start.25
  1187.0 2.2 copy-start.29
  1187.0 2.2 copy-start.31
  1187.1 3.5 copy-start.11
  1187.1 3.5 copy-start.18
  1187.1 688.7 %reduce-scatter.34.cloned.1.call-start = ((), (), s32[]{:S(2)}) async-start(), calls=%async_computation.18 | async-start | bytes 798720
  1189.2 907.0 %reduce-scatter.32.cloned.1.call-start = ((), (), s32[]{:S(2)}) async-start(), calls=%async_computation.17 | async-start | bytes 798720
  1190.5 1162.6 %reduce-scatter.40.cloned.1.call-start = ((), (), s32[]{:S(2)}) async-start(), calls=%async_computation.21 | async-start | bytes 27955200
  1202.1 1.0 copy-start.7
  1202.1 1.4 copy-start.13
  1202.2 1407.7 %reduce-scatter.38.cloned.1.call-start = ((), (), s32[]{:S(2)}) async-start(), calls=%async_computation.20 | async-start | bytes 27955200
  1214.5 1.3 copy-start.14
  1214.5 1651.9 %reduce-scatter.36.cloned.1.call-start = ((), (), s32[]{:S(2)}) async-start(), calls=%async_computation.19 | async-start | bytes 27955200
  1226.9 4.6 copy-start.5
  1231.5 2.3 copy-start.15
  1231.5 1634.9 %copy-start.1 = (bf16[6,128,1536]{2,1,0:T(8,128)(2,1)S(1)}, bf16[6,128,1536]{2,1,0:T(8,128)(2,1)}, u32[]{:S(2)}) copy-start(bf16[6,128,1536]{2,1,0:T(8,128)(2,1)} %param.33) | copy-start | bytes 7077892
  (5 other events, 3.2 us)
Sparse Core Ops, SparseCore 0:
  13.8 69.5 all-gather.3
  86.9 64.9 all-gather.5
  186.4 22.2 all-reduce.15
  260.8 26.1 all-reduce.17
  464.1 359.1 reduce-scatter.23
  825.6 352.3 reduce-scatter.25
  1181.1 20.7 all-reduce.19
  1207.5 223.2 reduce-scatter.29
  1436.5 218.9 reduce-scatter.27
  1660.8 214.8 reduce-scatter.33
  1881.2 214.9 reduce-scatter.31
  2102.2 250.8 reduce-scatter.39
  2359.2 250.6 reduce-scatter.37
  2615.9 250.5 reduce-scatter.35
where the time goes:
time: 2880 us; the launch traced here: 2870 us
  waiting for transfers between devices  2120 us (74%)
  blocking collectives  342 us (12%)
  matrix products  303 us (11%)
  other arithmetic  44.1 us (2%)
  local copies, waits for them, and re-layouts  39.4 us (1%)
    unnamed x19, waiting for transfers between devices  1210 us
    reduce_scatter x1, waiting for transfers between devices, local(): lax.psum_scatter(dv_acc, 'seq', scatter_dimension=0, tiled=True)  352 us
    reduce_scatter x1, waiting for transfers between devices, local(): lax.psum_scatter(dk_acc, 'seq', scatter_dimension=0, tiled=True)  348 us
    unnamed x1, blocking collectives  342 us
    reduce_scatter x1, waiting for transfers between devices, local(): lax.psum_scatter(d_w_query, 'seq', scatter_dimension=0, tiled=True)  73.5 us
    dot_general x48, matrix products, block_scores(): jnp.einsum('tkgd,skd->tkgs', query_rows, key_blk, preferred_element_type=...  63.2 us
    all_gather x1, waiting for transfers between devices, local(): lax.all_gather(key_rows, 'seq', axis=0, tiled=True)  57.7 us
  transfers between devices with their start and end apart: 14, of which 12 were waited for; matrix products, arithmetic and copies ran while one was open for 4% of the time, Pallas kernels for 0%

commit v1 on v0

v1 whole, which is shorter than its diff:
```python
import math

import jax
import jax.numpy as jnp
from jax import lax
from jax.experimental import pallas as pl
from jax.experimental.pallas import tpu as pltpu
from jax.sharding import PartitionSpec as P

MESH = pl.DeviceIdType.MESH
F32 = jnp.float32
BF16 = jnp.bfloat16
VMEM_BYTES = 60 * 1024 * 1024
AXES = ("z", "x", "y")
STRIDE = {"z": 16, "x": 4, "y": 1}


def coords():
    s = lax.axis_index("seq")
    return {"z": s // 16, "x": (s // 4) % 4, "y": s % 4}


def peer(axis, k):
    s = lax.axis_index("seq")
    c = coords()[axis]
    return (s + STRIDE[axis] * ((c + k) % 4 - c), lax.axis_index("tensor"))


def partner():
    return (lax.axis_index("seq"), 1 - lax.axis_index("tensor"))


def barrier(axes=AXES, core=False):
    bar = pltpu.get_barrier_semaphore()
    ids = [peer(a, k) for a in axes for k in (1, 2, 3)]
    if core:
        ids.append(partner())
    for d in ids:
        pl.semaphore_signal(bar, inc=1, device_id=d, device_id_type=MESH)
    pl.semaphore_wait(bar, len(ids))


def remote(src, dst, send, recv, device):
    return pltpu.make_async_remote_copy(
        src_ref=src, dst_ref=dst, send_sem=send, recv_sem=recv, device_id=device, device_id_type=MESH
    )


def comm_call(body, outs, ins, scratch, cid, name):
    vm = pl.BlockSpec(memory_space=pltpu.VMEM)
    return pl.pallas_call(
        body,
        out_shape=outs,
        in_specs=[vm] * ins,
        out_specs=jax.tree.map(lambda _: vm, outs),
        scratch_shapes=scratch,
        compiler_params=pltpu.CompilerParams(
            collective_id=cid, has_side_effects=True, vmem_limit_bytes=VMEM_BYTES
        ),
        name=name,
    )


DMA = pltpu.SemaphoreType.DMA


def core_sum(cid, *parts):
    n = len(parts)

    def body(*refs):
        ins, outs, bufs, send, recv = refs[:n], refs[n : 2 * n], refs[2 * n : 3 * n], refs[3 * n], refs[3 * n + 1]
        barrier((), True)
        copies = []
        for i in range(n):
            c = remote(ins[i], bufs[i], send.at[i], recv.at[i], partner())
            c.start()
            copies.append(c)
        for i in range(n):
            copies[i].wait()
            outs[i][...] = ins[i][...] + bufs[i][...]

    shapes = tuple(jax.ShapeDtypeStruct(p.shape, p.dtype) for p in parts)
    scratch = [pltpu.VMEM(p.shape, p.dtype) for p in parts] + [DMA((n,)), DMA((n,))]
    return comm_call(body, shapes, n, scratch, cid, "core_sum")(*parts)


KV_PARTS = (
    (0, 96, ("z", "x", "y")),
    (96, 80, ("x", "y", "z")),
    (176, 80, ("y", "z", "x")),
)


def kv_index(done, c, r0, rn):
    return tuple(slice(None) if a in done else c[a] for a in AXES) + (pl.ds(r0, rn), slice(None))


def gather_kv(kv):
    def body(kv_ref, out, send, recv):
        c = coords()
        out[c["z"], c["x"], c["y"]] = kv_ref[...]
        barrier()
        pending = [[] for _ in KV_PARTS]
        for stage in range(3):
            for p, (r0, rn, order) in enumerate(KV_PARTS):
                for copy in pending[p]:
                    copy.wait()
                pending[p] = []
                idx = kv_index(order[:stage], c, r0, rn)
                for k in (1, 2, 3):
                    src = kv_ref.at[pl.ds(r0, rn), :] if stage == 0 else out.at[idx]
                    n = (p * 3 + stage) * 3 + k - 1
                    copy = remote(src, out.at[idx], send.at[n], recv.at[n], peer(order[stage], k))
                    copy.start()
                    pending[p].append(copy)
        for copies in pending:
            for copy in copies:
                copy.wait()

    shape = jax.ShapeDtypeStruct((4, 4, 4, 256, 128), BF16)
    return comm_call(body, shape, 1, [DMA((27,)), DMA((27,))], 0, "gather_kv")(kv)


def scatter_kv(partial):
    def body(*refs):
        ins, out = refs[0], refs[1]
        got1, got2, got3 = refs[2:5], refs[5:8], refs[8:11]
        acc1, acc2 = refs[11:14], refs[14:17]
        send, recv = refs[17], refs[18]
        c = coords()
        barrier()
        pending = [[] for _ in KV_PARTS]
        for stage in range(3):
            for p, (r0, rn, order) in enumerate(KV_PARTS):
                for copy in pending[p]:
                    copy.wait()
                pending[p] = []
                rest = [a for a in AXES if a not in order[:1]]
                if stage == 1:
                    own = ins[kv_index(rest, c, r0, rn)].astype(F32)
                    for k in range(3):
                        own = own + got1[p][k].astype(F32)
                    acc1[p][...] = own.astype(BF16)
                if stage == 2:
                    own = acc1[p][pick1(rest, order, c[order[1]])].astype(F32)
                    for k in range(3):
                        own = own + got2[p][k].astype(F32)
                    acc2[p][...] = own.astype(BF16)
                for k in (1, 2, 3):
                    there = (c[order[stage]] + k) % 4
                    if stage == 0:
                        cc = dict(c)
                        cc[order[0]] = there
                        src, dst = ins.at[kv_index(rest, cc, r0, rn)], got1[p].at[k - 1]
                    elif stage == 1:
                        src, dst = acc1[p].at[pick1(rest, order, there)], got2[p].at[k - 1]
                    else:
                        src, dst = acc2[p].at[there], got3[p].at[k - 1]
                    n = (p * 3 + stage) * 3 + k - 1
                    copy = remote(src, dst, send.at[n], recv.at[n], peer(order[stage], k))
                    copy.start()
                    pending[p].append(copy)
        for p, (r0, rn, order) in enumerate(KV_PARTS):
            for copy in pending[p]:
                copy.wait()
            own = acc2[p][c[order[2]]].astype(F32)
            for k in range(3):
                own = own + got3[p][k].astype(F32)
            out[pl.ds(r0, rn), :] = own

    def pick1(rest, order, where):
        return (where,) if rest[0] == order[1] else (slice(None), where)

    rows = [rn for _, rn, _ in KV_PARTS]
    scratch = (
        [pltpu.VMEM((3, 4, 4, r, 128), BF16) for r in rows]
        + [pltpu.VMEM((3, 4, r, 128), BF16) for r in rows]
        + [pltpu.VMEM((3, r, 128), BF16) for r in rows]
        + [pltpu.VMEM((4, 4, r, 128), BF16) for r in rows]
        + [pltpu.VMEM((4, r, 128), BF16) for r in rows]
        + [DMA((27,)), DMA((27,))]
    )
    shape = jax.ShapeDtypeStruct((256, 128), F32)
    return comm_call(body, shape, 1, scratch, 1, "scatter_kv")(partial)


Q_BLK = 16
BLK = Q_BLK * 64
SCALE = 1.0 / math.sqrt(128)


def doc_bounds(pos, len_ref):
    start = jnp.zeros_like(pos)
    end = jnp.int32(0)
    for j in range(8):
        end = end + len_ref[j]
        start = jnp.where(pos >= end, end, start)
    return start


def doc_start_scalar(pos, len_ref):
    start, end = jnp.int32(0), jnp.int32(0)
    for j in range(8):
        end = end + len_ref[j]
        start = jnp.where(pos >= end, end, start)
    return start


def doc_end_scalar(pos, len_ref):
    end, result = jnp.int32(0), jnp.int32(0)
    for j in range(8):
        result = jnp.where(pos >= end, end + len_ref[j], result)
        end = end + len_ref[j]
    return result


def attn_forward(q, kv, lengths):
    def body(len_ref, q_ref, kv_ref, out_ref, lse_ref):
        dev = lax.axis_index("seq")
        col = lax.broadcasted_iota(jnp.int32, (96, BLK), 1)
        key_off = (col % Q_BLK) * 64 + col // Q_BLK
        row_off = (lax.broadcasted_iota(jnp.int32, (96, 1), 0) % Q_BLK) * 64 + dev

        def q_step(qb, _):
            q_blk = q_ref[qb]
            pos_q = row_off + qb * BLK
            start_q = doc_bounds(pos_q, len_ref)
            lo = doc_start_scalar(qb * BLK + dev, len_ref) // BLK

            def k_step(kb, carry):
                m, l, acc = carry
                rows = pl.ds(pl.multiple_of(kb * Q_BLK, Q_BLK), Q_BLK)
                vrows = pl.ds(pl.multiple_of(128 + kb * Q_BLK, Q_BLK), Q_BLK)
                k_blk = kv_ref[:, rows, :].reshape(BLK, 128)
                v_blk = kv_ref[:, vrows, :].reshape(BLK, 128)
                s = lax.dot_general(q_blk, k_blk, (((1,), (1,)), ((), ())), preferred_element_type=F32)
                pos_k = key_off + kb * BLK
                vis = (pos_k <= pos_q) & (pos_k >= start_q)
                s = jnp.where(vis, s * SCALE, -1e30)
                m_new = jnp.maximum(m, jnp.max(s, axis=1, keepdims=True))
                p = jnp.where(vis, jnp.exp(s - m_new), 0.0)
                a = jnp.exp(m - m_new)
                l = l * a + jnp.sum(p, axis=1, keepdims=True)
                acc = acc * a + jnp.dot(p.astype(BF16), v_blk, preferred_element_type=F32)
                return m_new, l, acc

            init = (jnp.full((96, 1), -1e30, F32), jnp.zeros((96, 1), F32), jnp.zeros((96, 128), F32))
            m, l, acc = lax.fori_loop(lo, qb + 1, k_step, init)
            out_ref[qb] = acc / l
            lse_ref[qb] = m + jnp.log(l)
            return 0

        lax.fori_loop(0, 8, q_step, 0)

    vm = pl.BlockSpec(memory_space=pltpu.VMEM)
    return pl.pallas_call(
        body,
        out_shape=(jax.ShapeDtypeStruct((8, 96, 128), F32), jax.ShapeDtypeStruct((8, 96, 1), F32)),
        in_specs=[pl.BlockSpec(memory_space=pltpu.SMEM), vm, vm],
        out_specs=(vm, vm),
        compiler_params=pltpu.CompilerParams(vmem_limit_bytes=VMEM_BYTES),
        name="attn_forward",
    )(lengths, q, kv)


def attn_backward(q, g, kv, lse, delta, lengths):
    def body(len_ref, q_ref, g_ref, kv_ref, lse_ref, delta_ref, dq_ref, dkv_ref):
        dev = lax.axis_index("seq")
        row = lax.broadcasted_iota(jnp.int32, (BLK, 96), 0)
        key_off = (row % Q_BLK) * 64 + row // Q_BLK
        q_off = (lax.broadcasted_iota(jnp.int32, (1, 96), 1) % Q_BLK) * 64 + dev
        dq_ref[...] = jnp.zeros_like(dq_ref)

        def k_step(kb, _):
            rows = pl.ds(pl.multiple_of(kb * Q_BLK, Q_BLK), Q_BLK)
            vrows = pl.ds(pl.multiple_of(128 + kb * Q_BLK, Q_BLK), Q_BLK)
            k_blk = kv_ref[:, rows, :].reshape(BLK, 128)
            v_blk = kv_ref[:, vrows, :].reshape(BLK, 128)
            k_t = k_blk.T
            pos_k = key_off + kb * BLK
            hi = (doc_end_scalar(kb * BLK + BLK - 1, len_ref) - 1) // BLK

            def q_step(qb, carry):
                dk, dv = carry
                q_blk, g_blk = q_ref[qb], g_ref[qb]
                pos_q = q_off + qb * BLK
                start_q = doc_bounds(pos_q, len_ref)
                s = lax.dot_general(k_blk, q_blk, (((1,), (1,)), ((), ())), preferred_element_type=F32)
                vis = (pos_k <= pos_q) & (pos_k >= start_q)
                p = jnp.where(vis, jnp.exp(s * SCALE - lse_ref[qb]), 0.0)
                gp = lax.dot_general(v_blk, g_blk, (((1,), (1,)), ((), ())), preferred_element_type=F32)
                gs = (p * (gp - delta_ref[qb])).astype(BF16)
                dq_ref[qb] += jnp.dot(k_t, gs, preferred_element_type=F32)
                dk = dk + jnp.dot(gs, q_blk, preferred_element_type=F32)
                dv = dv + jnp.dot(p.astype(BF16), g_blk, preferred_element_type=F32)
                return dk, dv

            zero = jnp.zeros((BLK, 128), F32)
            dk, dv = lax.fori_loop(kb, hi + 1, q_step, (zero, zero))
            dkv_ref[:, rows, :] = (dk * SCALE).astype(BF16).reshape(64, Q_BLK, 128)
            dkv_ref[:, vrows, :] = dv.astype(BF16).reshape(64, Q_BLK, 128)
            return 0

        lax.fori_loop(0, 8, k_step, 0)

    vm = pl.BlockSpec(memory_space=pltpu.VMEM)
    return pl.pallas_call(
        body,
        out_shape=(jax.ShapeDtypeStruct((8, 128, 96), F32), jax.ShapeDtypeStruct((64, 256, 128), BF16)),
        in_specs=[pl.BlockSpec(memory_space=pltpu.SMEM)] + [vm] * 5,
        out_specs=(vm, vm),
        compiler_params=pltpu.CompilerParams(vmem_limit_bytes=VMEM_BYTES),
        name="attn_backward",
    )(lengths, q, g, kv, lse, delta)


def to_blocks(v):
    return v.reshape(8, Q_BLK, 6, 128).transpose(0, 2, 1, 3).reshape(8, 96, 128)


def from_blocks(v):
    return v.reshape(8, 6, Q_BLK, 128).transpose(0, 2, 1, 3).reshape(128, 768)


FF_BLK = 640


def nt(a, b):
    return lax.dot_general(a, b, (((1,), (1,)), ((), ())), preferred_element_type=F32)


def feed_forward(normed, cot, w_gate, w_up, w_down):
    ff = w_gate.shape[1]

    def body(n_ref, c_ref, wg_ref, wu_ref, wd_ref, out_ref, gn_ref, h_ref, gg_ref, gu_ref):
        n, c = n_ref[...], c_ref[...]
        gate = jnp.dot(n, wg_ref[...], preferred_element_type=F32)
        up = jnp.dot(n, wu_ref[...], preferred_element_type=F32)
        gh = nt(c, wd_ref[...])
        sig = 1.0 / (1.0 + jnp.exp(-gate))
        silu = gate * sig
        hidden = (silu * up).astype(BF16)
        g_gate = (gh * up * sig * (1.0 + gate * (1.0 - sig))).astype(BF16)
        g_up = (gh * silu).astype(BF16)
        h_ref[...], gg_ref[...], gu_ref[...] = hidden, g_gate, g_up
        first = pl.program_id(0) == 0
        add_o = jnp.dot(hidden, wd_ref[...], preferred_element_type=F32)
        add_g = nt(g_gate, wg_ref[...]) + nt(g_up, wu_ref[...])

        @pl.when(first)
        def _():
            out_ref[...] = add_o
            gn_ref[...] = add_g

        @pl.when(jnp.logical_not(first))
        def _():
            out_ref[...] += add_o
            gn_ref[...] += add_g

    rows = normed.shape[0]
    whole = pl.BlockSpec((rows, 1536), lambda i: (0, 0))
    cols = pl.BlockSpec((1536, FF_BLK), lambda i: (0, i))
    act = pl.BlockSpec((rows, FF_BLK), lambda i: (0, i))
    return pl.pallas_call(
        body,
        grid=(ff // FF_BLK,),
        out_shape=(
            jax.ShapeDtypeStruct((rows, 1536), F32),
            jax.ShapeDtypeStruct((rows, 1536), F32),
        )
        + (jax.ShapeDtypeStruct((rows, ff), BF16),) * 3,
        in_specs=[whole, whole, cols, cols, pl.BlockSpec((FF_BLK, 1536), lambda i: (i, 0))],
        out_specs=(whole, whole, act, act, act),
        compiler_params=pltpu.CompilerParams(vmem_limit_bytes=VMEM_BYTES),
        name="feed_forward",
    )(normed, cot, w_gate, w_up, w_down)


FC = 1152


def col_start(c):
    return pl.multiple_of(jnp.minimum(c * FC, 4480 - FC), 128)


MLP_AXES = (("z", "x", "y"), ("x", "y", "z"), ("y", "z", "x"))


def mlp_weight_grads(norm_t, cot_t, g_gate, g_up, hidden):
    def body(*refs):
        nt_ref, ct_ref = refs[0], refs[1]
        grads = refs[2:5]
        outs = refs[5:8]
        xs, gs = refs[8:11], refs[11:14]
        sendbuf, got1, got2, acc2, got3 = refs[14:17], refs[17:20], refs[20:23], refs[23:26], refs[26:29]
        loc, send, recv = refs[29], refs[30], refs[31]
        c = coords()
        barrier()
        left = (nt_ref, nt_ref, ct_ref)
        first = []
        for m in range(3):
            w = MLP_AXES[m][0]
            copies = []
            for k in (1, 2, 3):
                n = (m * 4) * 6 + (k - 1) * 2
                a = remote(left[m], xs[m].at[:, pl.ds(k * 128, 128)], send.at[n], recv.at[n], peer(w, k))
                b = remote(
                    grads[m].at[:, pl.ds(col_start((c[w] + k) % 4), FC)],
                    gs[m].at[pl.ds(k * 128, 128), :],
                    send.at[n + 1],
                    recv.at[n + 1],
                    peer(w, k),
                )
                a.start()
                b.start()
                copies += [a, b]
            a = pltpu.make_async_copy(left[m], xs[m].at[:, pl.ds(0, 128)], loc.at[2 * m])
            b = pltpu.make_async_copy(
                grads[m].at[:, pl.ds(col_start(c[w]), FC)], gs[m].at[pl.ds(0, 128), :], loc.at[2 * m + 1]
            )
            a.start()
            b.start()
            first.append(copies + [a, b])

        pending = [[], [], []]

        def send_slab(m, stage, k, src, dst):
            n = (m * 4 + stage) * 6 + k - 1
            copy = remote(src, dst, send.at[n], recv.at[n], peer(MLP_AXES[m][stage % 3], k))
            copy.start()
            pending[m].append(copy)

        def dot(x, g):
            return jnp.dot(x, g, preferred_element_type=F32)

        def regroup(v, outer, inner):
            return jnp.concatenate(
                [v[(o * inner + i) * 24 : (o * inner + i + 1) * 24] for i in range(inner) for o in range(outer)], axis=0
            )

        m = 0
        for copy in first[m]:
            copy.wait()
        for k in (1, 2, 3, 0):
            u = (c["x"] + k) % 4
            rows = [pl.ds(pl.multiple_of(z * 384 + u * 96, 32), 96) for z in range(4)]
            x = jnp.concatenate([xs[m][r, :] for r in rows], axis=0)
            sendbuf[m][k] = regroup(dot(x, gs[m][...]), 4, 4).astype(BF16)
            if k:
                send_slab(m, 1, k, sendbuf[m].at[k], got1[m].at[k - 1])
        m = 2
        for copy in first[m]:
            copy.wait()
        for k in (1, 2, 3, 0):
            u = (c["z"] + k) % 4
            x = xs[m][pl.ds(pl.multiple_of(u * 384, 128), 384), :]
            sendbuf[m][k] = dot(x, gs[m][...]).astype(BF16)
            if k:
                send_slab(m, 1, k, sendbuf[m].at[k], got1[m].at[k - 1])
        m = 1
        for copy in first[m]:
            copy.wait()
        for z in range(4):
            v = regroup(dot(xs[m][z * 384 : (z + 1) * 384, :], gs[m][...]), 4, 4).astype(BF16)
            for y in range(4):
                sendbuf[m][y, z * 96 : (z + 1) * 96] = v[y * 96 : (y + 1) * 96]
        for k in (1, 2, 3):
            send_slab(m, 1, k, sendbuf[m].at[(c["y"] + k) % 4], got1[m].at[k - 1])

        for m in (0, 2, 1):
            for copy in pending[m]:
                copy.wait()
            pending[m] = []
            own = c["y"] if m == 1 else 0
            total = sendbuf[m][own].astype(F32)
            for k in range(3):
                total = total + got1[m][k].astype(F32)
            sendbuf[m][own] = total.astype(BF16)
            axis = MLP_AXES[m][2]
            for k in (1, 2, 3):
                rows = pl.ds(pl.multiple_of(((c[axis] + k) % 4) * 96, 32), 96)
                send_slab(m, 2, k, sendbuf[m].at[own, rows, :], got2[m].at[k - 1])
        for m in (0, 2, 1):
            for copy in pending[m]:
                copy.wait()
            pending[m] = []
            own = c["y"] if m == 1 else 0
            rows = pl.ds(pl.multiple_of(c[MLP_AXES[m][2]] * 96, 32), 96)
            total = sendbuf[m][own, rows, :].astype(F32)
            for k in range(3):
                total = total + got2[m][k].astype(F32)
            acc2[m][...] = total
            axis = MLP_AXES[m][0]
            for k in (1, 2, 3):
                rows = pl.ds(pl.multiple_of(((c[axis] + k) % 4) * 24, 8), 24)
                send_slab(m, 3, k, acc2[m].at[rows, :], got3[m].at[k - 1])
        for m in (0, 2, 1):
            for copy in pending[m]:
                copy.wait()
            here = c[MLP_AXES[m][0]]
            outs[m][:, pl.ds(col_start(here), FC)] = acc2[m][pl.ds(pl.multiple_of(here * 24, 8), 24), :]
            for k in (1, 2, 3):
                outs[m][:, pl.ds(col_start((here + 4 - k) % 4), FC)] = got3[m][k - 1]

    scratch = (
        [pltpu.VMEM((1536, 512), BF16)] * 3
        + [pltpu.VMEM((512, FC), BF16)] * 3
        + [pltpu.VMEM((4, 384, FC), BF16)] * 3
        + [pltpu.VMEM((3, 384, FC), BF16)] * 3
        + [pltpu.VMEM((3, 96, FC), BF16)] * 3
        + [pltpu.VMEM((96, FC), F32)] * 3
        + [pltpu.VMEM((3, 24, FC), F32)] * 3
        + [DMA((6,)), DMA((72,)), DMA((72,))]
    )
    shape = tuple(jax.ShapeDtypeStruct((24, 4480), F32) for _ in range(3))
    return comm_call(body, shape, 5, scratch, 2, "mlp_weight_grads")(norm_t, cot_t, g_gate, g_up, hidden)


ATTN_PARTS = ((640, ("z", "x", "y")), (640, ("x", "y", "z")), (512, ("y", "z", "x")))
SMALL = 40


def attn_weight_grads(norm_t, branch_t, g_qkv, attn_low, small):
    def body(*refs):
        nt_ref, bt_ref, g_ref, a_ref, s_ref = refs[:5]
        outs, s_out = refs[5:8], refs[8]
        sendbuf, got1, got2, acc2, got3 = refs[9:12], refs[12:15], refs[15:18], refs[18:21], refs[21:24]
        s_acc, s_got, send, recv = refs[24:28]
        c = coords()
        barrier(core=True)
        s_copy = remote(s_ref, s_got.at[0], send.at[36], recv.at[36], partner())
        s_copy.start()
        pending = [[], [], []]

        def send_slab(p, stage, k, src, dst):
            n = (p * 3 + stage) * 3 + k - 1
            copy = remote(src, dst, send.at[n], recv.at[n], peer(ATTN_PARTS[p][1][stage], k))
            copy.start()
            pending[p].append(copy)

        def product(rows, p):
            x, b = nt_ref[rows, :], bt_ref[rows, :]
            if p == 0:
                return jnp.dot(x, g_ref[:, :640], preferred_element_type=F32)
            if p == 1:
                left = jnp.dot(x, g_ref[:, 640:], preferred_element_type=F32)
                return jnp.concatenate([left, jnp.dot(b, a_ref[:, :256], preferred_element_type=F32)], axis=1)
            return jnp.dot(b, a_ref[:, 256:], preferred_element_type=F32)

        def blocks(v, order):
            return jnp.concatenate([v[o * 24 : (o + 1) * 24] for o in order], axis=0)

        for z in range(4):
            rows = slice(z * 384, (z + 1) * 384)
            sendbuf[0][z] = product(rows, 0).astype(BF16)
        for z in range(4):
            rows = slice(z * 384, (z + 1) * 384)
            v = product(rows, 2)
            v = blocks(v, [x * 4 + y for y in range(4) for x in range(4)]).astype(BF16)
            for y in range(4):
                sendbuf[2][y, z * 96 : (z + 1) * 96] = v[y * 96 : (y + 1) * 96]
        for x in range(4):
            v = jnp.concatenate([product(slice(z * 384 + x * 96, z * 384 + (x + 1) * 96), 1) for z in range(4)], axis=0)
            sendbuf[1][x] = blocks(v, [z * 4 + y for y in range(4) for z in range(4)]).astype(BF16)
        for p in range(3):
            for k in (1, 2, 3):
                there = (c[ATTN_PARTS[p][1][0]] + k) % 4
                send_slab(p, 0, k, sendbuf[p].at[there], got1[p].at[k - 1])
        s_copy.wait()
        s_acc[0] = s_ref[...] + s_got[0]
        s_pending = []

        def send_small(stage):
            for k in (1, 2, 3):
                n = 27 + stage * 3 + k - 1
                copy = remote(
                    s_acc.at[stage], s_got.at[1 + stage * 3 + k - 1], send.at[n], recv.at[n], peer(AXES[stage], k)
                )
                copy.start()
                s_pending.append(copy)

        def sum_small(stage):
            for copy in s_pending:
                copy.wait()
            s_pending.clear()
            axis = AXES[stage]
            parts = [s_acc[stage]] + [s_got[1 + stage * 3 + k] for k in range(3)]
            total = jnp.zeros_like(parts[0])
            for w in range(4):
                term = jnp.zeros_like(total)
                for k in range(4):
                    term = jnp.where((c[axis] + 4 - k) % 4 == w, parts[k], term)
                total = total + term
            return total

        send_small(0)
        for p in range(3):
            for copy in pending[p]:
                copy.wait()
            pending[p] = []
            order = ATTN_PARTS[p][1]
            own = c[order[0]]
            total = sendbuf[p][own].astype(F32)
            for k in range(3):
                total = total + got1[p][k].astype(F32)
            sendbuf[p][own] = total.astype(BF16)
            for k in (1, 2, 3):
                rows = pl.ds(pl.multiple_of(((c[order[1]] + k) % 4) * 96, 32), 96)
                send_slab(p, 1, k, sendbuf[p].at[own, rows, :], got2[p].at[k - 1])
        s_acc[1] = sum_small(0)
        send_small(1)
        for p in range(3):
            for copy in pending[p]:
                copy.wait()
            pending[p] = []
            order = ATTN_PARTS[p][1]
            own = c[order[0]]
            rows = pl.ds(pl.multiple_of(c[order[1]] * 96, 32), 96)
            total = sendbuf[p][own, rows, :].astype(F32)
            for k in range(3):
                total = total + got2[p][k].astype(F32)
            acc2[p][...] = total
            for k in (1, 2, 3):
                rows = pl.ds(pl.multiple_of(((c[order[2]] + k) % 4) * 24, 8), 24)
                send_slab(p, 2, k, acc2[p].at[rows, :], got3[p].at[k - 1])
        s_acc[2] = sum_small(1)
        send_small(2)
        for p in range(3):
            for copy in pending[p]:
                copy.wait()
            rows = pl.ds(pl.multiple_of(c[ATTN_PARTS[p][1][2]] * 24, 8), 24)
            total = acc2[p][rows, :]
            for k in range(3):
                total = total + got3[p][k]
            outs[p][...] = total
        s_out[...] = sum_small(2)

    cols = [n for n, _ in ATTN_PARTS]
    scratch = (
        [pltpu.VMEM((4, 384, n), BF16) for n in cols]
        + [pltpu.VMEM((3, 384, n), BF16) for n in cols]
        + [pltpu.VMEM((3, 96, n), BF16) for n in cols]
        + [pltpu.VMEM((96, n), F32) for n in cols]
        + [pltpu.VMEM((3, 24, n), F32) for n in cols]
        + [pltpu.VMEM((3, SMALL, 128), F32), pltpu.VMEM((10, SMALL, 128), F32), DMA((37,)), DMA((37,))]
    )
    shape = tuple(jax.ShapeDtypeStruct((24, n), F32) for n in cols) + (jax.ShapeDtypeStruct((SMALL, 128), F32),)
    return comm_call(body, shape, 5, scratch, 3, "attn_weight_grads")(norm_t, branch_t, g_qkv, attn_low, small)


def inverse_rms(values):
    return lax.rsqrt(jnp.mean(values * values, axis=-1, keepdims=True) + 1e-06)


def rotate(values, cos_table, sin_table):
    front, back_half = values[..., :64], values[..., 64:]
    return jnp.concatenate(
        [front * cos_table - back_half * sin_table, back_half * cos_table + front * sin_table], axis=-1
    )


def rotate_back(gradient, cos_table, sin_table):
    front, back_half = gradient[..., :64], gradient[..., 64:]
    return jnp.concatenate(
        [front * cos_table + back_half * sin_table, back_half * cos_table - front * sin_table], axis=-1
    )


def norm_back(gradient, source, inverse, gain):
    scaled = gradient * gain
    return inverse * scaled - source * inverse**3 * jnp.mean(scaled * source, axis=-1, keepdims=True)


def dot(a, b):
    return jnp.dot(a, b, preferred_element_type=F32)


def local(
    tokens, cotangent, lengths, norm1_gain, w_query, b_query, w_key, b_key, w_value, b_value, w_out,
    norm2_gain, w_gate, w_up, w_down,
):
    device = lax.axis_index("seq")
    core = lax.axis_index("tensor")
    positions = jnp.arange(128, dtype=jnp.int32) * 64 + device
    doc_ends = jnp.cumsum(lengths)
    is_past = positions[:, None] >= doc_ends[None, :]
    doc_start = jnp.sum(jnp.where(is_past, lengths[None, :], 0), axis=1)
    inv_freq = jnp.exp(-(2.0 * jnp.arange(64, dtype=F32) / 128) * math.log(10000.0))
    angles = (positions - doc_start).astype(F32)[:, None] * inv_freq[None, :]
    cos_table, sin_table = jnp.cos(angles)[:, None, :], jnp.sin(angles)[:, None, :]

    inputs = tokens.astype(F32)
    inv_first = inverse_rms(inputs)
    normed_first = (inputs * inv_first * norm1_gain).astype(BF16)
    wq, wk, wv = w_query.reshape(1536, 768), w_key.reshape(1536, 128), w_value.reshape(1536, 128)
    q_pre = dot(normed_first, wq).reshape(128, 6, 128) + b_query.astype(F32)
    k_pre = dot(normed_first, wk).reshape(128, 1, 128) + b_key.astype(F32)
    v_pre = dot(normed_first, wv) + b_value.astype(F32)
    q_blocks = to_blocks(rotate(q_pre, cos_table, sin_table).astype(BF16).reshape(128, 768))
    key_rows = rotate(k_pre, cos_table, sin_table).astype(BF16).reshape(128, 128)
    kv = gather_kv(jnp.concatenate([key_rows, v_pre.astype(BF16)], axis=0)).reshape(64, 256, 128)

    attn_blocks, lse = attn_forward(q_blocks, kv, lengths)
    attn_low = from_blocks(attn_blocks.astype(BF16))
    wo = w_out.reshape(768, 1536)
    (branch,) = core_sum(4, dot(attn_low, wo))
    mid_stream = inputs + branch
    inv_second = inverse_rms(mid_stream)
    normed_second = (mid_stream * inv_second * norm2_gain).astype(BF16)

    mlp_part, g_normed2_part, hidden, g_gate, g_up = feed_forward(normed_second, cotangent, w_gate, w_up, w_down)
    d_norm2 = jnp.sum(g_normed2_part * mid_stream * inv_second, axis=0)
    mlp_out, g_normed2 = core_sum(5, mlp_part, g_normed2_part)
    output = mid_stream + mlp_out
    g_mid = cotangent.astype(F32) + norm_back(g_normed2, mid_stream, inv_second, norm2_gain)
    g_branch = g_mid.astype(BF16)

    grad_gate, grad_up, grad_down = mlp_weight_grads(normed_second.T, cotangent.T, g_gate, g_up, hidden)

    g_attn = nt(g_branch, wo)
    g_blocks = to_blocks(g_attn.astype(BF16))
    delta = jnp.sum(g_blocks.astype(F32) * attn_blocks, axis=-1)
    dq_t, dkv = attn_backward(
        q_blocks, g_blocks, kv, lse.reshape(8, 1, 96), delta.reshape(8, 1, 96), lengths
    )
    dkv_own = scatter_kv(dkv.reshape(4, 4, 4, 256, 128))
    dq = from_blocks(dq_t.transpose(0, 2, 1)).reshape(128, 6, 128) * SCALE
    g_q_pre = rotate_back(dq, cos_table, sin_table).astype(BF16).reshape(128, 768)
    g_k_pre = rotate_back(dkv_own[:128].reshape(128, 1, 128), cos_table, sin_table).astype(BF16).reshape(128, 128)
    g_v_pre = dkv_own[128:].astype(BF16)
    g_qkv = jnp.concatenate([g_q_pre, g_k_pre, g_v_pre], axis=1)
    d_bias = jnp.sum(g_qkv.astype(F32), axis=0)
    g_normed1_part = nt(g_q_pre, wq) + nt(g_k_pre, wk) + nt(g_v_pre, wv)
    d_norm1 = jnp.sum(g_normed1_part * inputs * inv_first, axis=0)
    (g_normed1,) = core_sum(6, g_normed1_part)
    grad_tokens = g_mid + norm_back(g_normed1, inputs, inv_first, norm1_gain)

    part0, part1, part2, sums = attn_weight_grads(
        normed_first.T, g_branch.T, g_qkv, attn_low, pack_small(d_norm1, d_norm2, d_bias, core)
    )
    sums = sums.reshape(-1)
    grad_wq = jnp.concatenate([part0, part1[:, :128]], axis=1).reshape(24, 6, 128)
    grad_wk = part1[:, 128:256].reshape(24, 1, 128)
    grad_wv = part1[:, 256:384].reshape(24, 1, 128)
    grad_wo = jnp.concatenate([part1[:, 384:], part2], axis=1).T.reshape(6, 128, 24)
    grad_norm1 = lax.dynamic_slice(sums, (device * 24,), (24,))
    grad_norm2 = lax.dynamic_slice(sums, (1536 + device * 24,), (24,))
    bias = lax.dynamic_slice(sums, (3072 + core * 1024,), (1024,)).reshape(8, 128)
    bias = lax.dynamic_slice(bias, (0, device * 2), (8, 2))
    return (
        output,
        grad_tokens,
        grad_norm1,
        grad_wq,
        bias[:6],
        grad_wk,
        bias[6:7],
        grad_wv,
        bias[7:8],
        grad_wo,
        grad_norm2,
        grad_gate,
        grad_up,
        grad_down.T,
    )


def pack_small(d_norm1, d_norm2, d_bias, core):
    zero = jnp.zeros_like(d_bias)
    return jnp.concatenate(
        [d_norm1, d_norm2, jnp.where(core == 0, d_bias, zero), jnp.where(core == 1, d_bias, zero)]
    ).reshape(SMALL, 128)


def solution(mesh):
    in_specs = (
        P("seq", None), P("seq", None), P(), P(), P(None, "tensor", None), P("tensor", None),
        P(None, "tensor", None), P("tensor", None), P(None, "tensor", None), P("tensor", None),
        P("tensor", None, None), P(), P(None, "tensor"), P(None, "tensor"), P("tensor", None),
    )
    out_specs = (
        P("seq", None), P("seq", None), P("seq"), P("seq", "tensor", None), P("tensor", "seq"),
        P("seq", "tensor", None), P("tensor", "seq"), P("seq", "tensor", None), P("tensor", "seq"),
        P("tensor", None, "seq"), P("seq"), P("seq", "tensor"), P("seq", "tensor"), P("tensor", "seq"),
    )
    return jax.shard_map(local, mesh=mesh, in_specs=in_specs, out_specs=out_specs, check_vma=False)
```

time: 2880 us -> 386 us (0.13)
  waiting for transfers between devices: 2120 us -> 0 us
  blocking collectives: 342 us -> 0 us
  Pallas kernels: 0 us -> 298 us
  matrix products: 303 us -> 11 us
    unnamed x19 -> x0, waiting for transfers between devices: 1210 us -> none
    reduce_scatter x4 -> x0, waiting for transfers between devices: 773 us -> none  [the longest x1 352 us: local(): lax.psum_scatter(dv_acc, 'seq', scatter_dimension=0, tiled=True)]
    unnamed x1 -> x0, blocking collectives: 342 us -> none
    pallas_call x0 -> x10, Pallas kernels: none -> 298 us  [the longest x1 106 us: mlp_weight_grads(): comm_call(body, shape, 5, scratch, 2, 'mlp_weight_grads')]
    dot_general x164 -> x8, matrix products: 301 us -> 11 us  [the longest x4 7.02 us: dot(): return jnp.dot(a, b, preferred_element_type=F32)]
    all_gather x2 -> x0, waiting for transfers between devices: 90.2 us -> none  [the longest x1 57.7 us: local(): lax.all_gather(key_rows, 'seq', axis=0, tiled=True)]
    psum x3 -> x0, waiting for transfers between devices: 48.2 us -> none  [the longest x1 26 us: local(): g_normed2 = lax.psum(g_normed2_part, 'tensor')]
  transfers between devices with their start and end apart: 14 -> 0, of which waited for: 12 -> 0; matrix products, arithmetic and copies ran while one was open for 4% -> 0% of each run, Pallas kernels for 0% -> 0%
where the time goes in v1:
time: 386 us; the launch traced here: 382 us
  Pallas kernels  298 us (77%)
  local copies, waits for them, and re-layouts  46 us (12%)
  other arithmetic  25.6 us (7%)
  matrix products  11 us (3%)
    pallas_call x1, Pallas kernels, mlp_weight_grads(): comm_call(body, shape, 5, scratch, 2, 'mlp_weight_grads')  106 us
    pallas_call x1, Pallas kernels, attn_weight_grads(): comm_call(body, shape, 5, scratch, 3, 'attn_weight_grads')  43 us
    pallas_call x1, Pallas kernels, scatter_kv(): return comm_call(body, shape, 1, scratch, 1, 'scatter_kv')(partial)  37.2 us
    pallas_call x1, Pallas kernels, gather_kv(): comm_call(body, shape, 1, [DMA((27,)), DMA((27,))], 0, 'gather_kv')(kv)  36.5 us
    pallas_call x1, Pallas kernels, feed_forward(): pl.pallas_call(body, grid=(ff // FF_BLK,), out_shape=(jax.ShapeDtypeStruc...  27.1 us
    pallas_call x1, Pallas kernels, attn_backward(): pl.pallas_call(body, out_shape=(jax.ShapeDtypeStruct((8, 128, 96), F32),...  21 us
    unnamed x66, local copies, waits for them, and re-layouts  19.3 us
    pallas_call x3, Pallas kernels, core_sum(): return comm_call(body, shapes, n, scratch, cid, 'core_sum')(*parts)  14.9 us

profile of v1, /device:TPU:0, one launch (start us, length us, event | category | flops | bytes accessed | tf_op | source)
XLA Modules:
  0.0 382.1 jit_solution(11305796952974994929)
XLA Ops:
  0.7 1.4 copy.93
  2.8 4.3 %copy.94 = bf16[1536,6,128]{0,2,1:T(8,128)(2,1)} copy(bf16[1536,6,128]{2,0,1:T(8,128)(2,1)} %param.19) | data formatting | bytes 4718592 | tf_op args[4]
  7.1 2.6 fusion.2
  12.1 1.5 fusion.5
  14.0 1.6 fusion.6
  16.3 36.5 %gather_kv.1 = bf16[4,4,4,256,128]{4,3,2,1,0:T(8,128)(2,1)} custom-call(bf16[256,128]{1,0:T(8,128)(2,1)} %pad_maximum_fusion.1.kv_ref), custom_call_target="tpu_custom_call" | custom-call | tf_op jit(solution)/shard_map/gather_kv/pallas_call | solution.py:121
  52.8 12.9 %attn_forward.1 = (f32[8,96,128]{2,1,0:T(8,128)}, f32[8,96,1]{2,1,0:T(8,128)}) custom-call(s32[8]{0:T(128)} %len_ref.3, bf16[8,96,128]{2,1,0:T(8,128)(2,1)} %bitcast.114, bf16[64,256,128]{2,1,0:T(8,128)(2,1)} %bitcast.109), custom_call_target="tpu_custom_call" | custom-call | tf_op jit(solution)/shard_map/attn_forward/pallas_call | solution.py:256
  65.7 1.0 convert_element_type.65
  67.5 1.4 fusion.55.refs_0_
  68.9 4.4 %core_sum.3 = f32[128,1536]{1,0:T(8,128)} custom-call(f32[128,1536]{1,0:T(8,128)} %fusion.55.refs_0_), custom_call_target="tpu_custom_call" | custom-call | tf_op jit(solution)/shard_map/core_sum/pallas_call | solution.py:84
  73.3 2.3 copy.101
  75.6 1.4 multiply_reduce_fusion.2
  77.5 1.0 fusion.60.refs_0_
  78.5 1.0 multiply_convert_fusion
  79.5 2.0 copy.102.n_ref
  81.5 27.1 %feed_forward.1 = (f32[128,1536]{1,0:T(8,128)}, f32[128,1536]{1,0:T(8,128)}, bf16[128,4480]{1,0:T(8,128)(2,1)}, bf16[128,4480]{1,0:T(8,128)(2,1)}, bf16[128,4480]{1,0:T(8,128)(2,1)}) custom-call(bf16[128,1536]{1,0:T(8,128)(2,1)} %copy.102.n_ref, bf16[128,1536]{1,0:T(8,128)(2,1)} %c_ref.1, bf16[1536,4480]{1,0:T(8,128)(2,1)} %wg_ref.1, ...), custom_call_target="tpu_custom_call" | custom-call | tf_op jit(solution)/shard_map/feed_forward/pallas_call | solution.py:364
  108.6 1.9 copy.104
  110.5 105.6 %mlp_weight_grads.1 = (f32[24,4480]{1,0:T(8,128)}, f32[24,4480]{1,0:T(8,128)}, f32[24,4480]{1,0:T(8,128)}) custom-call(bf16[1536,128]{1,0:T(8,128)(2,1)} %fusion.60.refs_0_, bf16[1536,128]{1,0:T(8,128)(2,1)} %bitcast.113, bf16[128,4480]{1,0:T(8,128)(2,1)} %get-tuple-element.44.refs_2_, bf16[128,4480]{1,0:T(8,128)(2,1)} %get-tuple-element.45.refs_3_, ...), custom_call_target="tpu_custom_call" | custom-call | tf_op jit(solution)/shard_map/mlp_weight_grads/pallas_call | solution.py:516
  216.1 6.1 %core_sum.4 = (f32[128,1536]{1,0:T(8,128)}, f32[128,1536]{1,0:T(8,128)}) custom-call(f32[128,1536]{1,0:T(8,128)} %get-tuple-element.33.refs_0_, f32[128,1536]{1,0:T(8,128)} %get-tuple-element.34.refs_1_), custom_call_target="tpu_custom_call" | custom-call | tf_op jit(solution)/shard_map/core_sum/pallas_call | solution.py:84
  222.2 2.4 copy.105
  224.6 2.3 copy.119
  226.9 2.5 multiply_reduce_fusion
  229.9 2.3 copy.103
  232.2 2.8 convert_bitcast_fusion
  235.9 0.9 convolution_convert_fusion
  236.8 0.9 reshape.324
  237.7 1.0 copy.106
  239.5 1.8 reduce
  241.3 21.0 %attn_backward.1 = (f32[8,128,96]{2,1,0:T(8,128)}, bf16[64,256,128]{2,1,0:T(8,128)(2,1)}) custom-call(s32[8]{0:T(128)} %len_ref.3, bf16[8,96,128]{2,1,0:T(8,128)(2,1)} %bitcast.115, bf16[8,96,128]{2,1,0:T(8,128)(2,1)} %bitcast.117, bf16[64,256,128]{2,1,0:T(8,128)(2,1)} %bitcast.110, f32[8,1,96]{2,1,0:T(1,128)} %bitcast.132, f32[8,1,96]{2,1,0:T(1,128)} %bitcast.131), custom_call_target="tpu_custom_call" | custom-call | tf_op jit(solution)/shard_map/attn_backward/pallas_call | solution.py:307
  262.4 1.1 multiply_bitcast_fusion
  263.5 0.9 copy.108
  264.4 1.0 copy.109
  266.6 1.0 multiply_add_fusion
  267.8 37.2 %scatter_kv.1 = f32[256,128]{1,0:T(8,128)} custom-call(bf16[4,4,4,256,128]{4,3,2,1,0:T(8,128)(2,1)} %bitcast.111), custom_call_target="tpu_custom_call" | custom-call | tf_op jit(solution)/shard_map/scatter_kv/pallas_call | solution.py:184
  308.5 2.5 convolution_bitcast_fusion
  311.7 1.2 copy.116.refs_0_
  312.8 4.4 %core_sum.5 = f32[128,1536]{1,0:T(8,128)} custom-call(f32[128,1536]{1,0:T(8,128)} %copy.116.refs_0_), custom_call_target="tpu_custom_call" | custom-call | tf_op jit(solution)/shard_map/core_sum/pallas_call | solution.py:84
  317.3 1.4 copy.117
  318.7 1.7 fusion.15
  320.4 1.3 maximum_bitcast_fusion.3.refs_4_
  321.7 2.0 fusion.46
  323.7 43.0 %attn_weight_grads.1 = (f32[24,640]{1,0:T(8,128)}, f32[24,640]{1,0:T(8,128)}, f32[24,512]{1,0:T(8,128)}, f32[40,128]{1,0:T(8,128)}) custom-call(bf16[1536,128]{1,0:T(8,128)(2,1)} %get-tuple-element.107.refs_0_, bf16[1536,128]{1,0:T(8,128)(2,1)} %get-tuple-element.98.refs_1_, bf16[128,1024]{1,0:T(8,128)(2,1)} %get-tuple-element.97.refs_2_, ...), custom_call_target="tpu_custom_call" | custom-call | tf_op jit(solution)/shard_map/attn_weight_grads/pallas_call | solution.py:648
  366.7 1.3 fusion.51
  372.9 1.4 fusion.52
  374.2 1.1 copy.122
  375.4 2.3 copy.121
  377.7 1.8 copy.150
  379.5 1.8 copy.151
  (99 shorter events, 18.6 us)
Async XLA Ops:
  0.6 66.2 %copy-start = (bf16[6,128,1536]{2,1,0:T(8,128)(2,1)S(1)}, bf16[6,128,1536]{2,1,0:T(8,128)(2,1)}, u32[]{:S(2)}) copy-start(bf16[6,128,1536]{2,1,0:T(8,128)(2,1)} %param.25) | copy-start | bytes 7077892
  2.8 11.2 %copy-start.23 = (f32[128]{0:T(128)}, f32[128]{0:T(128)S(1)}, u32[]{:S(2)}) copy-start(f32[128]{0:T(128)S(1)} %get-tuple-element.127) | copy-start | bytes 1540
  2.8 4.3 %copy-start.24 = (bf16[6,128]{1,0:T(8,128)(2,1)S(1)}, bf16[6,128]{1,0:T(8,128)(2,1)}, u32[]{:S(2)}) copy-start(bf16[6,128]{1,0:T(8,128)(2,1)} %param.20) | copy-start | bytes 4612
  2.8 4.3 %copy-start.15 = (f32[1536]{0:T(1024)S(1)}, f32[1536]{0:T(1024)}, u32[]{:S(2)}) copy-start(f32[1536]{0:T(1024)} %param.18) | copy-start | bytes 18436
  7.1 2.6 copy-start.22
  7.1 5.0 %copy-start.25 = (bf16[1,128]{1,0:T(2,128)(2,1)S(1)}, bf16[1,128]{1,0:T(2,128)(2,1)}, u32[]{:S(2)}) copy-start(bf16[1,128]{1,0:T(2,128)(2,1)} %param.22) | copy-start | bytes 772
  9.7 4.3 %copy-start.26 = (bf16[1,128]{1,0:T(2,128)(2,1)S(1)}, bf16[1,128]{1,0:T(2,128)(2,1)}, u32[]{:S(2)}) copy-start(bf16[1,128]{1,0:T(2,128)(2,1)} %param.24) | copy-start | bytes 772
  10.0 6.3 %copy-start.18 = (f32[128]{0:T(128)}, f32[128]{0:T(128)S(1)}, u32[]{:S(2)}) copy-start(f32[128]{0:T(128)S(1)} %subtract_convert_fusion.1) | copy-start | bytes 1540
  10.0 6.3 %copy-start.20 = (f32[64]{0:T(128)}, f32[64]{0:T(128)S(1)}, u32[]{:S(2)}) copy-start(f32[64]{0:T(128)S(1)} %multiply_exponential_fusion) | copy-start | bytes 772
  10.2 0.6 copy-start.12
  10.2 0.6 copy-start.13
  66.8 0.7 copy-start.6
  68.9 8.6 %copy-start.14 = (f32[1536]{0:T(1024)S(1)}, f32[1536]{0:T(1024)}, u32[]{:S(2)}) copy-start(f32[1536]{0:T(1024)} %param.26) | copy-start | bytes 18436
  77.5 1.0 copy-start.17
  235.0 0.9 copy-start.2
  235.0 3.7 copy-start.7
  238.7 2.6 copy-start.5
  267.7 38.3 %copy-start.19 = (f32[128]{0:T(128)S(1)}, f32[128]{0:T(128)}, u32[]{:S(2)}) copy-start(f32[128]{0:T(128)} %copy-done.18) | copy-start | bytes 1540
  267.7 38.3 %copy-start.21 = (f32[64]{0:T(128)S(1)}, f32[64]{0:T(128)}, u32[]{:S(2)}) copy-start(f32[64]{0:T(128)} %copy-done.20) | copy-start | bytes 772
  308.5 2.5 copy-start.10
  308.5 2.9 copy-start.8
  308.5 2.9 copy-start.11
  311.7 1.2 copy-start.1
  312.8 7.6 %copy-start.16 = (f32[1536]{0:T(1024)S(1)}, f32[1536]{0:T(1024)}, u32[]{:S(2)}) copy-start(f32[1536]{0:T(1024)} %get-tuple-element.92) | copy-start | bytes 18436
  318.7 3.1 copy-start.3
  323.7 50.5 %copy-start.4 = (f32[128,1536]{0,1:T(8,128)S(1)}, f32[128,1536]{0,1:T(8,128)}, u32[]{:S(2)}) copy-start(f32[128,1536]{0,1:T(8,128)} %get-tuple-element.108) | copy-start | bytes 2359300
  375.4 5.9 %copy-start.9 = (f32[24,4480]{1,0:T(8,128)S(1)}, f32[24,4480]{1,0:T(8,128)}, u32[]{:S(2)}) copy-start(f32[24,4480]{1,0:T(8,128)} %get-tuple-element.49) | copy-start | bytes 1290244

commit v2 on v1

v2 whole, which is shorter than its diff:
```python
import math

import jax
import jax.numpy as jnp
from jax import lax
from jax.experimental import pallas as pl
from jax.experimental.pallas import tpu as pltpu
from jax.sharding import PartitionSpec as P

MESH = pl.DeviceIdType.MESH
F32 = jnp.float32
BF16 = jnp.bfloat16
VMEM_BYTES = 60 * 1024 * 1024
AXES = ("z", "x", "y")
STRIDE = {"z": 16, "x": 4, "y": 1}


def coords():
    s = lax.axis_index("seq")
    return {"z": s // 16, "x": (s // 4) % 4, "y": s % 4}


def peer(axis, k):
    s = lax.axis_index("seq")
    c = coords()[axis]
    return (s + STRIDE[axis] * ((c + k) % 4 - c), lax.axis_index("tensor"))


def partner():
    return (lax.axis_index("seq"), 1 - lax.axis_index("tensor"))


def barrier(axes=AXES, core=False):
    bar = pltpu.get_barrier_semaphore()
    ids = [peer(a, k) for a in axes for k in (1, 2, 3)]
    if core:
        ids.append(partner())
    for d in ids:
        pl.semaphore_signal(bar, inc=1, device_id=d, device_id_type=MESH)
    pl.semaphore_wait(bar, len(ids))


def remote(src, dst, send, recv, device):
    return pltpu.make_async_remote_copy(
        src_ref=src, dst_ref=dst, send_sem=send, recv_sem=recv, device_id=device, device_id_type=MESH
    )


def comm_call(body, outs, ins, scratch, cid, name):
    vm = pl.BlockSpec(memory_space=pltpu.VMEM)
    return pl.pallas_call(
        body,
        out_shape=outs,
        in_specs=[vm] * ins,
        out_specs=jax.tree.map(lambda _: vm, outs),
        scratch_shapes=scratch,
        compiler_params=pltpu.CompilerParams(
            collective_id=cid, has_side_effects=True, vmem_limit_bytes=VMEM_BYTES
        ),
        name=name,
    )


DMA = pltpu.SemaphoreType.DMA


KV_PARTS = (
    (0, 96, ("z", "x", "y")),
    (96, 80, ("x", "y", "z")),
    (176, 80, ("y", "z", "x")),
)


def kv_index(done, c, r0, rn):
    return tuple(slice(None) if a in done else c[a] for a in AXES) + (pl.ds(r0, rn), slice(None))


def rope_tables(len_ref):
    lane = lax.broadcasted_iota(jnp.int32, (128, 128), 1)
    pos = lax.broadcasted_iota(jnp.int32, (128, 128), 0) * 64 + lax.axis_index("seq")
    rel = (pos - doc_bounds(pos, len_ref)).astype(F32)
    inv_freq = jnp.exp(-(2.0 * (lane % 64).astype(F32) / 128) * math.log(10000.0))
    angle = rel * inv_freq
    sin = jnp.sin(angle)
    return jnp.cos(angle), jnp.where(lane < 64, -sin, sin)


def swap_halves(v):
    return pltpu.roll(v, 64, 1)


def qkv_gather(tokens, gain, wq, wk, wv, bq, bk, bv, lengths):
    def body(len_ref, t_ref, g_ref, wq_ref, wk_ref, wv_ref, bq_ref, bk_ref, bv_ref,
             q_out, out, nt_out, cos_out, sin_out, send, recv):
        c = coords()
        x = t_ref[...].astype(F32)
        inv = lax.rsqrt(jnp.mean(x * x, axis=1, keepdims=True) + 1e-06)
        normed = (x * inv * g_ref[...]).astype(BF16)
        cos, sin = rope_tables(len_ref)
        cos_out[...], sin_out[...] = cos, sin
        k_pre = jnp.dot(normed, wk_ref[...], preferred_element_type=F32) + bk_ref[...].astype(F32)
        v_pre = jnp.dot(normed, wv_ref[...], preferred_element_type=F32) + bv_ref[...].astype(F32)
        k_rot = (k_pre * cos + swap_halves(k_pre) * sin).astype(BF16)
        out[c["z"], c["x"], c["y"]] = jnp.concatenate([k_rot, v_pre.astype(BF16)], axis=0)
        barrier()
        pending = [[] for _ in KV_PARTS]

        def send_stage(stage):
            for p, (r0, rn, order) in enumerate(KV_PARTS):
                for copy in pending[p]:
                    copy.wait()
                pending[p] = []
                idx = kv_index(order[:stage], c, r0, rn)
                for k in (1, 2, 3):
                    n = (p * 3 + stage) * 3 + k - 1
                    copy = remote(out.at[idx], out.at[idx], send.at[n], recv.at[n], peer(order[stage], k))
                    copy.start()
                    pending[p].append(copy)

        send_stage(0)
        for h in range(6):
            q = jnp.dot(normed, wq_ref[h], preferred_element_type=F32) + bq_ref[h : h + 1, :].astype(F32)
            q = (q * cos + swap_halves(q) * sin).astype(BF16)
            q_out[:, h * Q_BLK : (h + 1) * Q_BLK, :] = q.reshape(8, Q_BLK, 128)
        send_stage(1)
        nt_out[...] = normed.T
        send_stage(2)
        for copies in pending:
            for copy in copies:
                copy.wait()

    vm, sm = pl.BlockSpec(memory_space=pltpu.VMEM), pl.BlockSpec(memory_space=pltpu.SMEM)
    return pl.pallas_call(
        body,
        out_shape=(
            jax.ShapeDtypeStruct((8, 96, 128), BF16),
            jax.ShapeDtypeStruct((4, 4, 4, 256, 128), BF16),
            jax.ShapeDtypeStruct((1536, 128), BF16),
            jax.ShapeDtypeStruct((128, 128), F32),
            jax.ShapeDtypeStruct((128, 128), F32),
        ),
        in_specs=[sm] + [vm] * 8,
        out_specs=(vm,) * 5,
        scratch_shapes=[DMA((27,)), DMA((27,))],
        compiler_params=pltpu.CompilerParams(collective_id=0, has_side_effects=True, vmem_limit_bytes=VMEM_BYTES),
        name="qkv_gather",
    )(lengths, tokens, gain, wq, wk, wv, bq, bk, bv)


Q_BLK = 16
BLK = Q_BLK * 64
SCALE = 1.0 / math.sqrt(128)


def doc_bounds(pos, len_ref):
    start = jnp.zeros_like(pos)
    end = jnp.int32(0)
    for j in range(8):
        end = end + len_ref[j]
        start = jnp.where(pos >= end, end, start)
    return start


def doc_start_scalar(pos, len_ref):
    start, end = jnp.int32(0), jnp.int32(0)
    for j in range(8):
        end = end + len_ref[j]
        start = jnp.where(pos >= end, end, start)
    return start


def attn_forward(q, kv, w_out, lengths):
    def body(len_ref, q_ref, kv_ref, wo_ref, part_ref, out_ref, low_ref, lse_ref):
        dev = lax.axis_index("seq")
        col = lax.broadcasted_iota(jnp.int32, (96, BLK), 1)
        key_off = (col % Q_BLK) * 64 + col // Q_BLK
        row_off = (lax.broadcasted_iota(jnp.int32, (96, 1), 0) % Q_BLK) * 64 + dev

        def q_step(qb, _):
            q_blk = q_ref[qb]
            pos_q = row_off + qb * BLK
            start_q = doc_bounds(pos_q, len_ref)
            lo = doc_start_scalar(qb * BLK + dev, len_ref) // BLK

            def k_step(kb, carry):
                m, l, acc = carry
                rows = pl.ds(pl.multiple_of(kb * Q_BLK, Q_BLK), Q_BLK)
                vrows = pl.ds(pl.multiple_of(128 + kb * Q_BLK, Q_BLK), Q_BLK)
                k_blk = kv_ref[:, rows, :].reshape(BLK, 128)
                v_blk = kv_ref[:, vrows, :].reshape(BLK, 128)
                s = lax.dot_general(q_blk, k_blk, (((1,), (1,)), ((), ())), preferred_element_type=F32)
                pos_k = key_off + kb * BLK
                vis = (pos_k <= pos_q) & (pos_k >= start_q)
                s = jnp.where(vis, s * SCALE, -1e30)
                m_new = jnp.maximum(m, jnp.max(s, axis=1, keepdims=True))
                p = jnp.where(vis, jnp.exp(s - m_new), 0.0)
                a = jnp.exp(m - m_new)
                l = l * a + jnp.sum(p, axis=1, keepdims=True)
                acc = acc * a + jnp.dot(p.astype(BF16), v_blk, preferred_element_type=F32)
                return m_new, l, acc

            init = (jnp.full((96, 1), -1e30, F32), jnp.zeros((96, 1), F32), jnp.zeros((96, 128), F32))
            m, l, acc = lax.fori_loop(lo, qb + 1, k_step, init)
            attn = acc / l
            out_ref[qb] = attn
            low = attn.astype(BF16)
            for h in range(6):
                rows = pl.ds(pl.multiple_of(qb * Q_BLK, Q_BLK), Q_BLK)
                low_ref[rows, h * 128 : (h + 1) * 128] = low[h * Q_BLK : (h + 1) * Q_BLK]
            lse_ref[qb] = jnp.broadcast_to(m + jnp.log(l), (96, 128)).T[0:1]
            return 0

        lax.fori_loop(0, 8, q_step, 0)
        part_ref[...] = jnp.dot(low_ref[...], wo_ref[...], preferred_element_type=F32)

    vm = pl.BlockSpec(memory_space=pltpu.VMEM)
    return pl.pallas_call(
        body,
        out_shape=(
            jax.ShapeDtypeStruct((128, 1536), F32),
            jax.ShapeDtypeStruct((8, 96, 128), F32),
            jax.ShapeDtypeStruct((128, 768), BF16),
            jax.ShapeDtypeStruct((8, 1, 96), F32),
        ),
        in_specs=[pl.BlockSpec(memory_space=pltpu.SMEM), vm, vm, vm],
        out_specs=(vm,) * 4,
        compiler_params=pltpu.CompilerParams(vmem_limit_bytes=VMEM_BYTES),
        name="attn_forward",
    )(lengths, q, kv, w_out)


FC = 1152


def nt(a, b):
    return lax.dot_general(a, b, (((1,), (1,)), ((), ())), preferred_element_type=F32)


def mm(a, b):
    return jnp.dot(a, b, preferred_element_type=F32)


def col_start(c):
    return pl.multiple_of(jnp.minimum(c * FC, 4480 - FC), 128)


MLP_AXES = (("z", "x", "y"), ("x", "y", "z"), ("y", "z", "x"))


def feed_forward(branch, attn, tokens, cot, gain, w_out, w_gate, w_up, w_down):
    def body(br_ref, at_ref, t_ref, c_ref, g_ref, wo_ref, wg_hbm, wu_hbm, wd_hbm,
             out_ref, gmid_ref, bt_ref, ga_ref, delta_ref, dn_ref, x0, x1, x2, g0, g1, g2,
             wg, wu, wd, got_br, acc, got, mid_ref, norm_ref, nt_ref, act, w_sem, loc, send, recv):
        xs, gs = (x0, x1, x2), (g0, g1, g2)
        c = coords()
        turn = c["z"] + c["x"] + c["y"]
        sems = iter(range(64))

        def load(j):
            cols = pl.ds(col_start((turn + j) % 4), FC)
            b = j % 2
            copies = [
                pltpu.make_async_copy(wg_hbm.at[:, cols], wg.at[b], w_sem.at[b, 0]),
                pltpu.make_async_copy(wu_hbm.at[:, cols], wu.at[b], w_sem.at[b, 1]),
                pltpu.make_async_copy(wd_hbm.at[cols, :], wd.at[b], w_sem.at[b, 2]),
            ]
            for copy in copies:
                copy.start()
            return copies

        loads = [load(0), load(1)]
        barrier(core=True)

        def push(src, dst, device):
            n = next(sems)
            copy = remote(src, dst, send.at[n], recv.at[n], device)
            copy.start()
            return copy

        later = []
        ex = push(br_ref, got_br, partner())
        x2[:, 0:128] = c_ref[...].T
        for k in (1, 2, 3):
            later.append(push(x2.at[:, pl.ds(0, 128)], x2.at[:, pl.ds(k * 128, 128)], peer("y", k)))
        ex.wait()
        mid = t_ref[...].astype(F32) + (br_ref[...] + got_br[...])
        mid_ref[...] = mid
        inv = lax.rsqrt(jnp.mean(mid * mid, axis=1, keepdims=True) + 1e-06)
        normed = (mid * inv * g_ref[...]).astype(BF16)
        norm_ref[...] = normed
        nt_ref[...] = normed.T
        x0[:, 0:128] = nt_ref[...]
        x1[:, 0:128] = nt_ref[...]
        for k in (1, 2, 3):
            for m, w in ((0, "z"), (1, "x")):
                later.append(push(nt_ref, xs[m].at[:, pl.ds(k * 128, 128)], peer(w, k)))

        lane = lax.broadcasted_iota(jnp.int32, (128, FC), 1)
        for j in range(4):
            b = j % 2
            d = (turn + j) % 4
            for copy in loads[j]:
                copy.wait()
            n = norm_ref[...]
            gate = mm(n, wg[b])
            up = mm(n, wu[b])
            gh = nt(c_ref[...], wd[b])
            sig = 1.0 / (1.0 + jnp.exp(-gate))
            silu = gate * sig
            hidden = (silu * up).astype(BF16)
            g_gate = (gh * up * sig * (1.0 + gate * (1.0 - sig))).astype(BF16)
            g_up = (gh * silu).astype(BF16)
            vals = (g_gate, g_up, hidden)
            for m in range(3):
                act[m, j] = vals[m]
            twice = (lane < 128) & (d == 3)
            zero = jnp.zeros((128, FC), BF16)
            hidden, g_gate, g_up = (jnp.where(twice, zero, v) for v in (hidden, g_gate, g_up))
            add_o = mm(hidden, wd[b])
            add_g = nt(g_gate, wg[b]) + nt(g_up, wu[b])
            if j == 0:
                acc[0], acc[1] = add_o, add_g
            else:
                acc[0] += add_o
                acc[1] += add_g
            if j + 2 < 4:
                loads.append(load(j + 2))
            for m in range(3):
                w = MLP_AXES[m][0]
                k = (d + 4 - c[w]) % 4
                slot = pl.ds(pl.multiple_of(k * 128, 128), 128)

                @pl.when(k == 0)
                def _():
                    copy = pltpu.make_async_copy(act.at[m, j], gs[m].at[pl.ds(0, 128), :], loc.at[m])
                    copy.start()
                    copy.wait()

                @pl.when(k != 0)
                def _():
                    remote(
                        act.at[m, j], gs[m].at[slot, :], send.at[32 + m * 4 + j], recv.at[32 + m * 4 + k], peer(w, k)
                    ).start()

        dn_ref[...] = jnp.sum(acc[1] * mid_ref[...] * inv, axis=0, keepdims=True)
        ex = [push(acc.at[1], got.at[1], partner()), push(acc.at[0], got.at[0], partner())]
        cot_f = c_ref[...].astype(F32)
        ex[0].wait()
        gn = acc[1] + got[1]
        mid = mid_ref[...]
        scaled = gn * g_ref[...]
        g_mid = cot_f + (inv * scaled - mid * (inv * inv * inv) * jnp.mean(scaled * mid, axis=1, keepdims=True))
        gmid_ref[...] = g_mid
        branch_low = g_mid.astype(BF16)
        bt_ref[...] = branch_low.T
        g_attn = nt(branch_low, wo_ref[...]).astype(BF16)
        for h in range(6):
            ga_ref[:, h * Q_BLK : (h + 1) * Q_BLK, :] = g_attn[:, h * 128 : (h + 1) * 128].reshape(8, Q_BLK, 128)
        for qb in range(8):
            delta_ref[qb] = jnp.sum((ga_ref[qb].astype(F32) * at_ref[qb]).T, axis=0, keepdims=True)
        ex[1].wait()
        out_ref[...] = mid_ref[...] + (acc[0] + got[0])
        for copy in later:
            copy.wait()
        for m in range(3):
            w = MLP_AXES[m][0]
            for j in range(4):
                k = ((turn + j) % 4 + 4 - c[w]) % 4

                @pl.when(k != 0)
                def _():
                    slot = pl.ds(pl.multiple_of(k * 128, 128), 128)
                    remote(
                        act.at[m, j], gs[m].at[slot, :], send.at[32 + m * 4 + j], recv.at[32 + m * 4 + k], peer(w, k)
                    ).wait()

    f32 = lambda *s: jax.ShapeDtypeStruct(s, F32)
    b16 = lambda *s: jax.ShapeDtypeStruct(s, BF16)
    vm, hbm = pl.BlockSpec(memory_space=pltpu.VMEM), pl.BlockSpec(memory_space=pl.ANY)
    return pl.pallas_call(
        body,
        out_shape=(f32(128, 1536), f32(128, 1536), b16(1536, 128), b16(8, 96, 128), f32(8, 1, 96), f32(1, 1536))
        + (b16(1536, 512),) * 3
        + (b16(512, FC),) * 3,
        in_specs=[vm] * 6 + [hbm] * 3,
        out_specs=(vm,) * 12,
        scratch_shapes=[
            pltpu.VMEM((2, 1536, FC), BF16),
            pltpu.VMEM((2, 1536, FC), BF16),
            pltpu.VMEM((2, FC, 1536), BF16),
            pltpu.VMEM((128, 1536), F32),
            pltpu.VMEM((2, 128, 1536), F32),
            pltpu.VMEM((2, 128, 1536), F32),
            pltpu.VMEM((128, 1536), F32),
            pltpu.VMEM((128, 1536), BF16),
            pltpu.VMEM((1536, 128), BF16),
            pltpu.VMEM((3, 4, 128, FC), BF16),
            DMA((2, 3)),
            DMA((3,)),
            DMA((64,)),
            DMA((64,)),
        ],
        compiler_params=pltpu.CompilerParams(collective_id=4, has_side_effects=True, vmem_limit_bytes=VMEM_BYTES),
        name="feed_forward",
    )(branch, attn, tokens, cot, gain, w_out, w_gate, w_up, w_down)


def backward(xs_in, gs_in, q, g, kv, lse, delta, lengths):
    def body(*refs):
        len_ref = refs[0]
        xs, gs = refs[1:4], refs[4:7]
        q_ref, g_ref, kv_ref, lse_ref, delta_ref = refs[7:12]
        outs, dq_ref, own_ref = refs[12:15], refs[15], refs[16]
        sendbuf, got1, got2, acc2, got3 = refs[17:20], refs[20:23], refs[23:26], refs[26:29], refs[29:32]
        dkv = refs[32]
        kv1, kv2, kv3, kva1, kva2 = refs[33:36], refs[36:39], refs[39:42], refs[42:45], refs[45:48]
        send, recv = refs[48], refs[49]
        c = coords()
        barrier()
        pending = [[], [], []]

        def send_slab(m, stage, k, src, dst):
            n = (m * 3 + stage - 1) * 3 + k - 1
            copy = remote(src, dst, send.at[n], recv.at[n], peer(MLP_AXES[m][stage % 3], k))
            copy.start()
            pending[m].append(copy)

        def regroup(v, outer, inner):
            return jnp.concatenate(
                [v[(o * inner + i) * 24 : (o * inner + i + 1) * 24] for i in range(inner) for o in range(outer)], axis=0
            )

        m = 0
        for k in (1, 2, 3, 0):
            u = (c["x"] + k) % 4
            rows = [pl.ds(pl.multiple_of(z * 384 + u * 96, 32), 96) for z in range(4)]
            x = jnp.concatenate([xs[m][r, :] for r in rows], axis=0)
            sendbuf[m][k] = regroup(mm(x, gs[m][...]), 4, 4).astype(BF16)
            if k:
                send_slab(m, 1, k, sendbuf[m].at[k], got1[m].at[k - 1])
        m = 2
        for k in (1, 2, 3, 0):
            u = (c["z"] + k) % 4
            x = xs[m][pl.ds(pl.multiple_of(u * 384, 128), 384), :]
            sendbuf[m][k] = mm(x, gs[m][...]).astype(BF16)
            if k:
                send_slab(m, 1, k, sendbuf[m].at[k], got1[m].at[k - 1])
        m = 1
        for z in range(4):
            v = regroup(mm(xs[m][z * 384 : (z + 1) * 384, :], gs[m][...]), 4, 4).astype(BF16)
            for y in range(4):
                sendbuf[m][y, z * 96 : (z + 1) * 96] = v[y * 96 : (y + 1) * 96]
        for k in (1, 2, 3):
            send_slab(m, 1, k, sendbuf[m].at[(c["y"] + k) % 4], got1[m].at[k - 1])

        dev = lax.axis_index("seq")
        row = lax.broadcasted_iota(jnp.int32, (BLK, 96), 0)
        key_off = (row % Q_BLK) * 64 + row // Q_BLK
        q_off = (lax.broadcasted_iota(jnp.int32, (1, 96), 1) % Q_BLK) * 64 + dev
        dq_ref[...] = jnp.zeros_like(dq_ref)

        def k_step(kb, _):
            rows = pl.ds(pl.multiple_of(kb * Q_BLK, Q_BLK), Q_BLK)
            vrows = pl.ds(pl.multiple_of(128 + kb * Q_BLK, Q_BLK), Q_BLK)
            k_blk = kv_ref[:, rows, :].reshape(BLK, 128)
            v_blk = kv_ref[:, vrows, :].reshape(BLK, 128)
            k_t = k_blk.T
            pos_k = key_off + kb * BLK

            def q_step(qb, carry):
                dk, dv = carry
                q_blk, g_blk = q_ref[qb], g_ref[qb]
                pos_q = q_off + qb * BLK
                start_q = doc_bounds(pos_q, len_ref)
                s = nt(k_blk, q_blk)
                vis = (pos_k <= pos_q) & (pos_k >= start_q)
                p = jnp.where(vis, jnp.exp(s * SCALE - lse_ref[qb]), 0.0)
                gp = nt(v_blk, g_blk)
                ds = (p * (gp - delta_ref[qb])).astype(BF16)
                dq_ref[qb] += mm(k_t, ds)
                dk = dk + mm(ds, q_blk)
                dv = dv + mm(p.astype(BF16), g_blk)
                return dk, dv

            zero = jnp.zeros((BLK, 128), F32)
            dk, dv = lax.fori_loop(kb, 8, q_step, (zero, zero))
            dkv[:, :, :, rows, :] = (dk * SCALE).astype(BF16).reshape(4, 4, 4, Q_BLK, 128)
            dkv[:, :, :, vrows, :] = dv.astype(BF16).reshape(4, 4, 4, Q_BLK, 128)
            return 0

        lax.fori_loop(0, 8, k_step, 0)

        kv_pending = [[] for _ in KV_PARTS]

        def pick1(rest, order, where):
            return (where,) if rest[0] == order[1] else (slice(None), where)

        def kv_stage(stage):
            for p, (r0, rn, order) in enumerate(KV_PARTS):
                for copy in kv_pending[p]:
                    copy.wait()
                kv_pending[p] = []
                rest = [a for a in AXES if a not in order[:1]]
                if stage == 1:
                    own = dkv[kv_index(rest, c, r0, rn)].astype(F32)
                    for k in range(3):
                        own = own + kv1[p][k].astype(F32)
                    kva1[p][...] = own.astype(BF16)
                if stage == 2:
                    own = kva1[p][pick1(rest, order, c[order[1]])].astype(F32)
                    for k in range(3):
                        own = own + kv2[p][k].astype(F32)
                    kva2[p][...] = own.astype(BF16)
                for k in (1, 2, 3):
                    there = (c[order[stage]] + k) % 4
                    if stage == 0:
                        cc = dict(c)
                        cc[order[0]] = there
                        src, dst = dkv.at[kv_index(rest, cc, r0, rn)], kv1[p].at[k - 1]
                    elif stage == 1:
                        src, dst = kva1[p].at[pick1(rest, order, there)], kv2[p].at[k - 1]
                    else:
                        src, dst = kva2[p].at[there], kv3[p].at[k - 1]
                    n = 27 + (p * 3 + stage) * 3 + k - 1
                    copy = remote(src, dst, send.at[n], recv.at[n], peer(order[stage], k))
                    copy.start()
                    kv_pending[p].append(copy)

        def mlp_second():
            for m in (0, 2, 1):
                for copy in pending[m]:
                    copy.wait()
                pending[m] = []
                own = c["y"] if m == 1 else 0
                total = sendbuf[m][own].astype(F32)
                for k in range(3):
                    total = total + got1[m][k].astype(F32)
                sendbuf[m][own] = total.astype(BF16)
                axis = MLP_AXES[m][2]
                for k in (1, 2, 3):
                    rows = pl.ds(pl.multiple_of(((c[axis] + k) % 4) * 96, 32), 96)
                    send_slab(m, 2, k, sendbuf[m].at[own, rows, :], got2[m].at[k - 1])

        def mlp_third():
            for m in (0, 2, 1):
                for copy in pending[m]:
                    copy.wait()
                pending[m] = []
                own = c["y"] if m == 1 else 0
                rows = pl.ds(pl.multiple_of(c[MLP_AXES[m][2]] * 96, 32), 96)
                total = sendbuf[m][own, rows, :].astype(F32)
                for k in range(3):
                    total = total + got2[m][k].astype(F32)
                acc2[m][...] = total
                axis = MLP_AXES[m][0]
                for k in (1, 2, 3):
                    rows = pl.ds(pl.multiple_of(((c[axis] + k) % 4) * 24, 8), 24)
                    send_slab(m, 3, k, acc2[m].at[rows, :], got3[m].at[k - 1])

        kv_stage(0)
        mlp_second()
        kv_stage(1)
        mlp_third()
        kv_stage(2)
        for p, (r0, rn, order) in enumerate(KV_PARTS):
            for copy in kv_pending[p]:
                copy.wait()
            own = kva2[p][c[order[2]]].astype(F32)
            for k in range(3):
                own = own + kv3[p][k].astype(F32)
            own_ref[pl.ds(r0, rn), :] = own
        for m in (0, 2, 1):
            for copy in pending[m]:
                copy.wait()
            here = c[MLP_AXES[m][0]]
            outs[m][:, pl.ds(col_start(here), FC)] = acc2[m][pl.ds(pl.multiple_of(here * 24, 8), 24), :]
            for k in (1, 2, 3):
                outs[m][:, pl.ds(col_start((here + 4 - k) % 4), FC)] = got3[m][k - 1]

    rows = [rn for _, rn, _ in KV_PARTS]
    scratch = (
        [pltpu.VMEM((4, 384, FC), BF16)] * 3
        + [pltpu.VMEM((3, 384, FC), BF16)] * 3
        + [pltpu.VMEM((3, 96, FC), BF16)] * 3
        + [pltpu.VMEM((96, FC), F32)] * 3
        + [pltpu.VMEM((3, 24, FC), F32)] * 3
        + [pltpu.VMEM((4, 4, 4, 256, 128), BF16)]
        + [pltpu.VMEM((3, 4, 4, r, 128), BF16) for r in rows]
        + [pltpu.VMEM((3, 4, r, 128), BF16) for r in rows]
        + [pltpu.VMEM((3, r, 128), BF16) for r in rows]
        + [pltpu.VMEM((4, 4, r, 128), BF16) for r in rows]
        + [pltpu.VMEM((4, r, 128), BF16) for r in rows]
        + [DMA((54,)), DMA((54,))]
    )
    vm, sm = pl.BlockSpec(memory_space=pltpu.VMEM), pl.BlockSpec(memory_space=pltpu.SMEM)
    return pl.pallas_call(
        body,
        out_shape=tuple(jax.ShapeDtypeStruct((24, 4480), F32) for _ in range(3))
        + (jax.ShapeDtypeStruct((8, 128, 96), F32), jax.ShapeDtypeStruct((256, 128), F32)),
        in_specs=[sm] + [vm] * 11,
        out_specs=(vm,) * 5,
        scratch_shapes=scratch,
        compiler_params=pltpu.CompilerParams(collective_id=2, has_side_effects=True, vmem_limit_bytes=VMEM_BYTES),
        name="backward",
    )(lengths, *xs_in, *gs_in, q, g, kv, lse, delta)


ATTN_PARTS = (
    ("o", 0, 256, ("z", "x", "y")),
    ("o", 256, 512, ("x", "y", "z")),
    ("o", 512, 768, ("y", "z", "x")),
    ("g", 0, 384, ("z", "x", "y")),
    ("g", 384, 768, ("x", "y", "z")),
    ("g", 768, 1024, ("y", "z", "x")),
)
SMALL = 40


def finish(dq_t, dkv, cos, sin, norm_t, branch_t, attn_low, wq, wk, wv, tokens, gain, g_mid, d_norm2):
    np_ = len(ATTN_PARTS)

    def body(*refs):
        (dq_ref, dkv_ref, cos_ref, sin_ref, nt_ref, bt_ref, a_ref, wq_ref, wk_ref, wv_ref, t_ref, gain_ref,
         gmid_ref, dn2_ref) = refs[:14]
        gt_ref, gq_ref, gk_ref, gv_ref, go_ref, s_out = refs[14:20]
        r = refs[20:]
        sendbuf, got1, got2, acc2, got3 = (r[i * np_ : (i + 1) * np_] for i in range(5))
        s_acc, s_got, g_ref, part, got_part, send, recv = r[5 * np_ :]
        c = coords()
        core = lax.axis_index("tensor")
        barrier(core=True)
        pending = [[] for _ in ATTN_PARTS]

        def send_slab(p, stage, k, src, dst):
            n = (p * 3 + stage) * 3 + k - 1
            copy = remote(src, dst, send.at[n], recv.at[n], peer(ATTN_PARTS[p][3][stage], k))
            copy.start()
            pending[p].append(copy)

        def blocks(v, order):
            return jnp.concatenate([v[o * 24 : (o + 1) * 24] for o in order], axis=0)

        def first(p):
            side, lo, hi, order = ATTN_PARTS[p]
            left, right = (bt_ref, a_ref) if side == "o" else (nt_ref, g_ref)
            rhs = right[:, lo:hi]
            if order[0] == "z":
                for z in range(4):
                    sendbuf[p][z] = mm(left[z * 384 : (z + 1) * 384, :], rhs).astype(BF16)
            elif order[0] == "x":
                for x in range(4):
                    lhs = jnp.concatenate([left[z * 384 + x * 96 : z * 384 + (x + 1) * 96, :] for z in range(4)], axis=0)
                    sendbuf[p][x] = blocks(mm(lhs, rhs), [z * 4 + y for y in range(4) for z in range(4)]).astype(BF16)
            else:
                for z in range(4):
                    v = mm(left[z * 384 : (z + 1) * 384, :], rhs)
                    v = blocks(v, [x * 4 + y for y in range(4) for x in range(4)]).astype(BF16)
                    for y in range(4):
                        sendbuf[p][y, z * 96 : (z + 1) * 96] = v[y * 96 : (y + 1) * 96]
            for k in (1, 2, 3):
                there = (c[order[0]] + k) % 4
                send_slab(p, 0, k, sendbuf[p].at[there], got1[p].at[k - 1])

        for p in range(3):
            first(p)

        cos_t, sin_t = cos_ref[...], sin_ref[...]
        for qb in range(8):
            dq = dq_ref[qb].T * SCALE
            rows = slice(qb * Q_BLK, (qb + 1) * Q_BLK)
            cs, sn = cos_t[rows], sin_t[rows]
            for h in range(6):
                v = dq[h * Q_BLK : (h + 1) * Q_BLK]
                g_ref[rows, h * 128 : (h + 1) * 128] = (v * cs - swap_halves(v) * sn).astype(BF16)
        dk = dkv_ref[:128, :]
        g_ref[:, 768:896] = (dk * cos_t - swap_halves(dk) * sin_t).astype(BF16)
        g_ref[:, 896:] = dkv_ref[128:, :].astype(BF16)
        total = nt(g_ref[:, 768:896], wk_ref[...]) + nt(g_ref[:, 896:], wv_ref[...])
        for h in range(6):
            total = total + nt(g_ref[:, h * 128 : (h + 1) * 128], wq_ref[h])
        part[...] = total
        n = 9 * np_
        swap = remote(part, got_part, send.at[n], recv.at[n], partner())
        swap.start()
        for p in range(3, np_):
            first(p)

        inputs = t_ref[...].astype(F32)
        inv = lax.rsqrt(jnp.mean(inputs * inputs, axis=1, keepdims=True) + 1e-06)
        d_norm1 = jnp.sum(part[...] * inputs * inv, axis=0, keepdims=True)
        d_bias = jnp.sum(g_ref[...].astype(F32), axis=0, keepdims=True)
        for j in range(12):
            s_acc[0, j : j + 1, :] = d_norm1[:, j * 128 : (j + 1) * 128]
            s_acc[0, 12 + j : 13 + j, :] = dn2_ref[:, j * 128 : (j + 1) * 128]
        for j in range(8):
            v = d_bias[:, j * 128 : (j + 1) * 128]
            s_acc[0, 24 + j : 25 + j, :] = jnp.where(core == 0, v, 0.0)
            s_acc[0, 32 + j : 33 + j, :] = jnp.where(core == 1, v, 0.0)
        s_pending = []

        def send_small(stage):
            peers = [partner()] if stage == 0 else [peer(AXES[stage - 1], k) for k in (1, 2, 3)]
            for i, d in enumerate(peers):
                n = 9 * np_ + 1 + stage * 3 + i
                copy = remote(s_acc.at[stage], s_got.at[stage * 3 + i], send.at[n], recv.at[n], d)
                copy.start()
                s_pending.append(copy)

        def sum_small(stage):
            for copy in s_pending:
                copy.wait()
            s_pending.clear()
            if stage == 0:
                return s_acc[0] + s_got[0]
            axis = AXES[stage - 1]
            parts = [s_acc[stage]] + [s_got[stage * 3 + k] for k in range(3)]
            total = jnp.zeros_like(parts[0])
            for w in range(4):
                term = jnp.zeros_like(total)
                for k in range(4):
                    term = jnp.where((c[axis] + 4 - k) % 4 == w, parts[k], term)
                total = total + term
            return total

        send_small(0)
        swap.wait()
        g_norm = part[...] + got_part[...]
        scaled = g_norm * gain_ref[...]
        gt_ref[...] = gmid_ref[...] + (
            inv * scaled - inputs * (inv * inv * inv) * jnp.mean(scaled * inputs, axis=1, keepdims=True)
        )
        s_acc[1] = sum_small(0)
        send_small(1)
        for p in range(np_):
            for copy in pending[p]:
                copy.wait()
            pending[p] = []
            order = ATTN_PARTS[p][3]
            own = c[order[0]]
            total = sendbuf[p][own].astype(F32)
            for k in range(3):
                total = total + got1[p][k].astype(F32)
            sendbuf[p][own] = total.astype(BF16)
            for k in (1, 2, 3):
                rows = pl.ds(pl.multiple_of(((c[order[1]] + k) % 4) * 96, 32), 96)
                send_slab(p, 1, k, sendbuf[p].at[own, rows, :], got2[p].at[k - 1])
        s_acc[2] = sum_small(1)
        send_small(2)
        for p in range(np_):
            for copy in pending[p]:
                copy.wait()
            pending[p] = []
            order = ATTN_PARTS[p][3]
            own = c[order[0]]
            rows = pl.ds(pl.multiple_of(c[order[1]] * 96, 32), 96)
            total = sendbuf[p][own, rows, :].astype(F32)
            for k in range(3):
                total = total + got2[p][k].astype(F32)
            acc2[p][...] = total
            for k in (1, 2, 3):
                rows = pl.ds(pl.multiple_of(((c[order[2]] + k) % 4) * 24, 8), 24)
                send_slab(p, 2, k, acc2[p].at[rows, :], got3[p].at[k - 1])
        s_acc[3] = sum_small(2)
        send_small(3)
        for p in range(np_):
            for copy in pending[p]:
                copy.wait()
            side, lo, hi, order = ATTN_PARTS[p]
            rows = pl.ds(pl.multiple_of(c[order[2]] * 24, 8), 24)
            total = acc2[p][rows, :]
            for k in range(3):
                total = total + got3[p][k]
            for j in range(lo // 128, hi // 128):
                v = total[:, j * 128 - lo : (j + 1) * 128 - lo]
                if side == "o":
                    go_ref[j] = v
                elif j < 6:
                    gq_ref[j] = v
                elif j == 6:
                    gk_ref[...] = v
                else:
                    gv_ref[...] = v
        s_out[...] = sum_small(3)

    cols = [hi - lo for _, lo, hi, _ in ATTN_PARTS]
    n_sem = 9 * np_ + 1 + 12
    scratch = (
        [pltpu.VMEM((4, 384, n), BF16) for n in cols]
        + [pltpu.VMEM((3, 384, n), BF16) for n in cols]
        + [pltpu.VMEM((3, 96, n), BF16) for n in cols]
        + [pltpu.VMEM((96, n), F32) for n in cols]
        + [pltpu.VMEM((3, 24, n), F32) for n in cols]
        + [
            pltpu.VMEM((4, SMALL, 128), F32),
            pltpu.VMEM((12, SMALL, 128), F32),
            pltpu.VMEM((128, 1024), BF16),
            pltpu.VMEM((128, 1536), F32),
            pltpu.VMEM((128, 1536), F32),
            DMA((n_sem,)),
            DMA((n_sem,)),
        ]
    )
    f32 = lambda *s: jax.ShapeDtypeStruct(s, F32)
    shape = (f32(128, 1536), f32(6, 24, 128), f32(24, 128), f32(24, 128), f32(6, 24, 128), f32(SMALL, 128))
    return comm_call(body, shape, 14, scratch, 3, "finish")(
        dq_t, dkv, cos, sin, norm_t, branch_t, attn_low, wq, wk, wv, tokens, gain, g_mid, d_norm2
    )


def local(
    tokens, cotangent, lengths, norm1_gain, w_query, b_query, w_key, b_key, w_value, b_value, w_out,
    norm2_gain, w_gate, w_up, w_down,
):
    device = lax.axis_index("seq")
    core = lax.axis_index("tensor")
    wq = w_query.transpose(1, 0, 2)
    wk, wv = w_key.reshape(1536, 128), w_value.reshape(1536, 128)
    wo = w_out.reshape(768, 1536)
    gain1, gain2 = norm1_gain.reshape(1, 1536), norm2_gain.reshape(1, 1536)

    q, kv, norm_t, cos, sin = qkv_gather(tokens, gain1, wq, wk, wv, b_query, b_key, b_value, lengths)
    kv = kv.reshape(64, 256, 128)
    branch, attn, attn_low, lse = attn_forward(q, kv, wo, lengths)
    output, g_mid, branch_t, g_attn, delta, d_norm2, *shared = feed_forward(
        branch, attn, tokens, cotangent, gain2, wo, w_gate, w_up, w_down
    )
    grad_gate, grad_up, grad_down, dq_t, dkv = backward(
        shared[:3], shared[3:], q, g_attn, kv, lse, delta, lengths
    )
    grad_tokens, grad_wq, grad_wk, grad_wv, grad_wo, sums = finish(
        dq_t, dkv, cos, sin, norm_t, branch_t, attn_low, wq, wk, wv, tokens, gain1, g_mid, d_norm2
    )
    sums = sums.reshape(-1)
    grad_norm1 = lax.dynamic_slice(sums, (device * 24,), (24,))
    grad_norm2 = lax.dynamic_slice(sums, (1536 + device * 24,), (24,))
    bias = lax.dynamic_slice(sums.reshape(SMALL, 128), (24 + core * 8, device * 2), (8, 2))
    return (
        output,
        grad_tokens,
        grad_norm1,
        grad_wq.transpose(1, 0, 2),
        bias[:6],
        grad_wk.reshape(24, 1, 128),
        bias[6:7],
        grad_wv.reshape(24, 1, 128),
        bias[7:8],
        grad_wo.transpose(0, 2, 1),
        grad_norm2,
        grad_gate,
        grad_up,
        grad_down.T,
    )


def solution(mesh):
    in_specs = (
        P("seq", None), P("seq", None), P(), P(), P(None, "tensor", None), P("tensor", None),
        P(None, "tensor", None), P("tensor", None), P(None, "tensor", None), P("tensor", None),
        P("tensor", None, None), P(), P(None, "tensor"), P(None, "tensor"), P("tensor", None),
    )
    out_specs = (
        P("seq", None), P("seq", None), P("seq"), P("seq", "tensor", None), P("tensor", "seq"),
        P("seq", "tensor", None), P("tensor", "seq"), P("seq", "tensor", None), P("tensor", "seq"),
        P("tensor", None, "seq"), P("seq"), P("seq", "tensor"), P("seq", "tensor"), P("tensor", "seq"),
    )
    return jax.shard_map(local, mesh=mesh, in_specs=in_specs, out_specs=out_specs, check_vma=False)
```

time: 386 us -> 247 us (0.64)
  Pallas kernels: 298 us -> 233 us
  local copies, waits for them, and re-layouts: 46 us -> 13 us
  other arithmetic: 25.6 us -> 0 us
  matrix products: 11 us -> 0 us
    pallas_call x10 -> x5, Pallas kernels: 298 us -> 233 us  [the longest x1 90.5 us: backward(): pl.pallas_call(body, out_shape=tuple((jax.ShapeDtypeStruct((24, 4480), F3...]
    dot_general x8 -> x0, matrix products: 11 us -> none  [the longest x4 7.02 us: dot(): return jnp.dot(a, b, preferred_element_type=F32)]
    unnamed x66 -> x28, local copies, waits for them, and re-layouts: 19.3 us -> 8.37 us
    pallas_call x5 -> x0, local copies, waits for them, and re-layouts: 10.6 us -> none  [the longest x4 8.32 us: core_sum(): return comm_call(body, shapes, n, scratch, cid, 'core_sum')(*parts)]
    reduce_sum x7 -> x0, other arithmetic: 7.46 us -> none  [the longest x1 2.48 us: local(): d_norm2 = jnp.sum(g_normed2_part * mid_stream * inv_second, axis=0)]
    transpose x4 -> x0, other arithmetic: 6 us -> none  [the longest x2 4.84 us: local(): part0, part1, part2, sums = attn_weight_grads(normed_first.T, g_branch.T,...]
where the time goes in v2:
time: 247 us
  Pallas kernels  233 us (94%)
  local copies, waits for them, and re-layouts  13 us (5%)
    pallas_call x1, Pallas kernels, backward(): pl.pallas_call(body, out_shape=tuple((jax.ShapeDtypeStruct((24, 4480), F3...  90.5 us
    pallas_call x1, Pallas kernels, feed_forward(): pl.pallas_call(body, out_shape=(f32(128, 1536), f32(128, 1536), b16(1536,...  45.5 us
    pallas_call x1, Pallas kernels, finish(): comm_call(body, shape, 14, scratch, 3, 'finish')  41.6 us
    pallas_call x1, Pallas kernels, qkv_gather(): pl.pallas_call(body, out_shape=(jax.ShapeDtypeStruct((8, 96, 128), BF16),...  38.5 us
    pallas_call x1, Pallas kernels, attn_forward(): pl.pallas_call(body, out_shape=(jax.ShapeDtypeStruct((128, 1536), F32), j...  16.7 us
    unnamed x28, local copies, waits for them, and re-layouts  8.37 us

profile of v2, /device:TPU:0, one launch (start us, length us, event | category | flops | bytes accessed | tf_op | source)
XLA Modules:
  0.0 246.5 jit_solution(6990230384044698988)
XLA Ops:
  0.6 1.3 reshape.55.g_ref.refs_11_
  1.9 38.5 %qkv_gather.1 = (bf16[8,96,128]{2,1,0:T(8,128)(2,1)}, bf16[4,4,4,256,128]{4,3,2,1,0:T(8,128)(2,1)}, bf16[1536,128]{1,0:T(8,128)(2,1)}, f32[128,128]{1,0:T(8,128)}, f32[128,128]{1,0:T(8,128)}) custom-call(s32[8]{0:T(128)} %refs_0_.1, bf16[128,1536]{1,0:T(8,128)(2,1)} %refs_10_.1, f32[1,1536]{1,0:T(1,128)} %reshape.55.g_ref.refs_11_, ...), custom_call_target="tpu_custom_call" | custom-call | tf_op jit(solution)/shard_map/qkv_gather/pallas_call | solution.py:133
  40.4 0.0 copy-start.8
  40.4 16.7 %attn_forward.1 = (f32[128,1536]{1,0:T(8,128)}, f32[8,96,128]{2,1,0:T(8,128)}, bf16[128,768]{1,0:T(8,128)(2,1)}, f32[8,1,96]{2,1,0:T(1,128)}) custom-call(s32[8]{0:T(128)} %refs_0_.1, bf16[8,96,128]{2,1,0:T(8,128)(2,1)} %get-tuple-element.46.q_ref.refs_7_, bf16[64,256,128]{2,1,0:T(8,128)(2,1)} %bitcast.16, bf16[768,1536]{1,0:T(8,128)(2,1)} %bitcast.18), custom_call_target="tpu_custom_call" | custom-call | tf_op jit(solution)/shard_map/attn_forward/pallas_call | solution.py:217
  57.1 0.0 copy-done.8
  57.1 0.6 reshape.60.g_ref
  57.7 45.5 %feed_forward.1 = (f32[128,1536]{1,0:T(8,128)}, f32[128,1536]{1,0:T(8,128)}, bf16[1536,128]{1,0:T(8,128)(2,1)}, bf16[8,96,128]{2,1,0:T(8,128)(2,1)}, f32[8,1,96]...) custom-call(f32[128,1536]{1,0:T(8,128)} %get-tuple-element.48.br_ref, ...), custom_call_target="tpu_custom_call" | custom-call | tf_op jit(solution)/shard_map/feed_forward/pallas_call | solution.py:380
  103.2 90.5 %backward.1 = (f32[24,4480]{1,0:T(8,128)}, f32[24,4480]{1,0:T(8,128)}, f32[24,4480]{1,0:T(8,128)}, f32[8,128,96]{2,1,0:T(8,128)}, f32[256,128]{1,0:T(8,128)}) custom-call(s32[8]{0:T(128)} %refs_0_.1, bf16[1536,512]{1,0:T(8,128)(2,1)} %get-tuple-element.51.refs_1_, bf16[1536,512]{1,0:T(8,128)(2,1)} %get-tuple-element.52.refs_2_, ...), custom_call_target="tpu_custom_call" | custom-call | tf_op jit(solution)/shard_map/backward/pallas_call | solution.py:596
  193.8 0.0 copy-start
  193.8 41.6 %finish.1 = (f32[128,1536]{1,0:T(8,128)}, f32[6,24,128]{2,1,0:T(8,128)}, f32[24,128]{1,0:T(8,128)}, f32[24,128]{1,0:T(8,128)}, f32[6,24,128]{2,1,0:T(8,128)}, /*index=5*/f32[40,128]{1,0:T(8,128)}) custom-call(f32[8,128,96]{2,1,0:T(8,128)} %get-tuple-element.60.refs_0_, f32[256,128]{1,0:T(8,128)} %get-tuple-element.61.refs_1_, ...), custom_call_target="tpu_custom_call" | custom-call | tf_op jit(solution)/shard_map/finish/pallas_call | solution.py:805
  235.4 0.0 copy-start.5
  235.4 0.0 copy-start.7
  235.4 0.0 copy-start.6
  235.4 0.0 copy-start.4
  235.4 0.0 copy-start.3
  235.4 0.0 copy-start.2
  235.5 0.8 dynamic_slice.10
  236.3 0.5 fusion.1
  236.8 0.6 copy.29
  237.5 1.4 fusion
  238.8 0.0 copy-done
  238.8 0.0 copy-start.1
  238.8 0.9 copy.41
  239.7 2.1 copy.42
  241.8 0.0 copy-done.5
  241.8 0.6 copy.43
  242.4 0.0 copy-done.7
  242.4 0.6 copy.44
  243.0 0.0 copy-done.6
  243.0 0.6 copy.45
  243.6 0.0 copy-done.4
  243.6 0.6 copy.46
  244.2 0.0 copy-done.3
  244.3 0.8 copy.47
  245.0 0.0 copy-done.2
  245.0 0.8 copy.48
  245.8 0.0 copy-done.1
  245.8 0.8 copy.49
Async XLA Ops:
  40.4 16.7 %copy-start.8 = (f32[1536]{0:T(1024)S(1)}, f32[1536]{0:T(1024)}, u32[]{:S(2)}) copy-start(f32[1536]{0:T(1024)} %param.26) | copy-start | bytes 18436
  193.8 45.0 %copy-start = (f32[128,1536]{1,0:T(8,128)S(1)}, f32[128,1536]{1,0:T(8,128)}, u32[]{:S(2)}) copy-start(f32[128,1536]{1,0:T(8,128)} %get-tuple-element.110) | copy-start | bytes 2359300
  235.4 6.4 %copy-start.5 = (f32[6,24,128]{2,1,0:T(8,128)S(1)}, f32[6,24,128]{2,1,0:T(8,128)}, u32[]{:S(2)}) copy-start(f32[6,24,128]{2,1,0:T(8,128)} %get-tuple-element.71) | copy-start | bytes 221188
  235.4 7.0 %copy-start.7 = (f32[24,128]{1,0:T(8,128)S(1)}, f32[24,128]{1,0:T(8,128)}, u32[]{:S(2)}) copy-start(f32[24,128]{1,0:T(8,128)} %get-tuple-element.72) | copy-start | bytes 36868
  235.4 7.6 %copy-start.6 = (f32[24,128]{1,0:T(8,128)S(1)}, f32[24,128]{1,0:T(8,128)}, u32[]{:S(2)}) copy-start(f32[24,128]{1,0:T(8,128)} %get-tuple-element.73) | copy-start | bytes 36868
  235.4 8.2 %copy-start.4 = (f32[6,24,128]{2,1,0:T(8,128)S(1)}, f32[6,24,128]{2,1,0:T(8,128)}, u32[]{:S(2)}) copy-start(f32[6,24,128]{2,1,0:T(8,128)} %get-tuple-element.74) | copy-start | bytes 221188
  235.4 8.8 %copy-start.3 = (f32[24,4480]{1,0:T(8,128)S(1)}, f32[24,4480]{1,0:T(8,128)}, u32[]{:S(2)}) copy-start(f32[24,4480]{1,0:T(8,128)} %get-tuple-element.121) | copy-start | bytes 1290244
  235.4 9.6 %copy-start.2 = (f32[24,4480]{1,0:T(8,128)S(1)}, f32[24,4480]{1,0:T(8,128)}, u32[]{:S(2)}) copy-start(f32[24,4480]{1,0:T(8,128)} %get-tuple-element.122) | copy-start | bytes 1290244
  238.8 7.0 %copy-start.1 = (f32[24,4480]{1,0:T(8,128)S(1)}, f32[24,4480]{1,0:T(8,128)}, u32[]{:S(2)}) copy-start(f32[24,4480]{1,0:T(8,128)} %get-tuple-element.77) | copy-start | bytes 1290244
